TPU v7x, 128 devices: a whole 4x4x4 slice. The times are simulated.
128 devices in a mesh: seq: 8 (over x, core), head: 16 (over y, z).
Axes of the slice: x: 4, y: 4, z: 4, core: 2. Of those that a mesh axis runs over, the one named last changes fastest.
Arguments:
- qk_in: bfloat16 [4, 8192, 2, 2048], P(None, 'seq', None, 'head'), may hold values from -6 to 6
- v_in: bfloat16 [4, 8192, 4096], P(None, 'seq', 'head'), may hold values from -6 to 6
- gate_z: bfloat16 [4, 8192, 4096], P(None, 'seq', 'head'), may hold values from -6 to 6
- conv_qk: bfloat16 [4, 2, 2048], P(None, None, 'head'), may hold values from -3 to 3
- conv_v: bfloat16 [4, 4096], P(None, 'head'), may hold values from -3 to 3
- log_decay: float32 [4, 32, 8192], P(None, 'head', 'seq'), may hold values from -0.7 to 0
- write_gain: float32 [4, 32, 8192], P(None, 'head', 'seq'), may hold values from 0 to 1
- norm_gain: float32 [128], replicated, may hold values from 0.5 to 1.5
- prompt_lengths: int32 [4], replicated, may hold values from 1 to 8192, 20480 in all
- placement: int32 [8, 16], P('seq'), may hold values from 0 to 3
Outputs:
- attended: bfloat16 [4, 8192, 4096], P(None, 'seq', 'head')
- rollout_state: float32 [8, 16, 32, 128, 128], P('seq', 'head')
Inputs may be any that keep to these rules, and one draw needn't show every extreme that they name: `prompt_lengths`: the largest length is exactly 8192; the lengths sum to 20480. Device (s, r) serves prompt placement[s, r]; the values 0 and 3 each occur at least once.
All inputs are finite; a program needn't handle non-finite values.
Results may differ from a plain program's by a relative error of at most 0.02.
Values may be sent and summed in bfloat16 or wider, within the bound.
A program may use at most 128 MiB of HBM per device.

v0:
```python
import functools

import jax
import jax.numpy as jnp
from jax import lax
from jax.experimental import pallas as pl
from jax.experimental.pallas import tpu as pltpu
from jax.sharding import PartitionSpec as P

DK = 128
DV = 128
CONV = 4
BLOCK = 128
BASE = 16
UNROLL = 4
RIM = 8
EPSILON = 1e-06
F32 = jnp.float32
BF16 = jnp.bfloat16
VMEM_LIMIT = 56 * 1024 * 1024


def dot(a, b):
    return jnp.dot(a, b, preferred_element_type=F32)


def silu(x):
    half = 0.5 * x
    return half + half * jnp.tanh(half)


def unit_inverses(stricts):
    lane = lax.broadcasted_iota(jnp.int32, (BASE, BLOCK), 1)
    row = lax.broadcasted_iota(jnp.int32, (BASE, BLOCK), 0)
    home = lane // BASE
    count = BLOCK // BASE
    lows = [s.astype(BF16) for s in stricts]
    compact = []
    for s in stricts:
        c = s[0:BASE]
        for b in range(1, count):
            c = jnp.where(home == b, s[b * BASE : (b + 1) * BASE], c)
        compact.append(c)
    eye = jnp.where(lane % BASE == row, 1.0, 0.0).astype(F32)
    xs = [eye for _ in stricts]
    for j in range(BASE - 1):
        index = home * BASE + j
        for n, c in enumerate(compact):
            column = jnp.take_along_axis(c, index, axis=1)
            xs[n] = xs[n] - column * xs[n][j : j + 1]
    slabs = []
    for x in xs:
        slabs.append([jnp.where(home == b, x, 0.0).astype(BF16) for b in range(count)])
    size = BASE
    while size < BLOCK:
        per = size // BASE
        lane_slab = lax.broadcasted_iota(jnp.int32, (size, BLOCK), 1) // size
        odd = [o for o in range(1, BLOCK // size, 2)]
        lefts = [
            jnp.concatenate([slab for o in odd for slab in sl[o * per : (o + 1) * per]], axis=0)
            for sl in slabs
        ]
        wholes = [jnp.concatenate(sl, axis=0) for sl in slabs]
        keep = jnp.concatenate([(lane_slab == o - 1).astype(F32) for o in odd], axis=0) > 0.5
        ys = [jnp.where(keep, dot(a, low), 0.0).astype(BF16) for a, low in zip(lefts, lows)]
        zs = [dot(y, w) for y, w in zip(ys, wholes)]
        for n, z in enumerate(zs):
            new = (lefts[n].astype(F32) - z).astype(BF16)
            for m, o in enumerate(odd):
                for i in range(per):
                    at = m * size + i * BASE
                    slabs[n][o * per + i] = new[at : at + BASE]
        size *= 2
    return [jnp.concatenate(sl, axis=0) for sl in slabs]


def maps_kernel(
    first_ref,
    len_ref,
    qk_ref,
    v_ref,
    rim_ref,
    cqk_ref,
    cv_ref,
    ld_ref,
    wg_ref,
    m_ref,
    out_ref,
    st_ref,
    xqk,
    xv,
    rows,
    gates,
    aq,
    binp,
    base_out,
    carry,
):
    p = pl.program_id(0)
    prompts = pl.num_programs(0)
    tok = v_ref.shape[1]
    nblk = tok // BLOCK
    heads = ld_ref.shape[1]

    xqk[0:RIM, :] = rim_ref[0, 0:RIM, :].astype(F32)
    xqk[RIM:, :] = qk_ref[0].astype(F32)
    for h in range(heads):
        lanes = slice(h * DV, (h + 1) * DV)
        xv[h, 0:RIM, :] = rim_ref[0, (1 + h) * RIM : (2 + h) * RIM, :].astype(F32)
        xv[h, RIM:, :] = v_ref[0, :, lanes].astype(F32)

    position = lax.broadcasted_iota(jnp.int32, (heads, tok), 1) + first_ref[0]
    valid = position < len_ref[p]
    log_gate = jnp.where(valid, ld_ref[0], 0.0)
    gain = jnp.where(valid, wg_ref[0], 0.0)
    rows[...] = jnp.zeros_like(rows)
    for c in range(nblk):
        rows[8 * c : 8 * c + heads, :] = log_gate[:, c * BLOCK : (c + 1) * BLOCK]
        rows[8 * c + heads : 8 * c + 2 * heads, :] = gain[:, c * BLOCK : (c + 1) * BLOCK]
    before = lax.broadcasted_iota(jnp.int32, (BLOCK, BLOCK), 0)
    after = lax.broadcasted_iota(jnp.int32, (BLOCK, BLOCK), 1)
    upto = jnp.where(before <= after, 1.0, 0.0).astype(F32)
    raw_rows = rows[...]
    sums = jnp.dot(raw_rows, upto, precision=lax.Precision.HIGHEST, preferred_element_type=F32)
    kind = lax.broadcasted_iota(jnp.int32, raw_rows.shape, 0) % 8
    rows[...] = jnp.where(kind < heads, sums, raw_rows)

    lower = before >= after
    strictly = before > after
    taps_qk = cqk_ref[...].astype(F32)
    taps_v = cv_ref[...].astype(F32)

    def group(g, _):
        blocks = range(UNROLL)
        queries, keys, keys_t, values, tiles, columns = [], [], [], [], [], []
        for u in blocks:
            c = g * UNROLL + u
            start = c * BLOCK

            def mixed(which):
                total = None
                for i in range(CONV):
                    at = RIM + 2 * (start - (CONV - 1) + i) + which
                    term = xqk[pl.ds(at, BLOCK, stride=2), :] * taps_qk[i, which : which + 1, :]
                    total = term if total is None else total + term
                return silu(total)

            def unit(x):
                return x * lax.rsqrt(jnp.sum(x * x, axis=-1, keepdims=True) + EPSILON)

            q = unit(mixed(0))
            k = unit(mixed(1))
            queries.append(q.astype(BF16))
            keys.append(k.astype(BF16))
            keys_t.append(k.T.astype(BF16))
            vs = []
            for h in range(heads):
                total = None
                for i in range(CONV):
                    at = RIM + start - (CONV - 1) + i
                    term = xv[h, pl.ds(at, BLOCK), :] * taps_v[i : i + 1, h * DV : (h + 1) * DV]
                    total = term if total is None else total + term
                vs.append(silu(total).astype(BF16))
            values.append(vs)
            tile = rows[pl.ds(pl.multiple_of(8 * c, 8), 8), :]
            tiles.append(tile)
            columns.append(tile.T)
        grams = [
            dot(jnp.concatenate([queries[u], keys[u]], axis=0), keys_t[u]) for u in blocks
        ]
        stricts, scores, fades, gains = [], [], [], []
        for u in blocks:
            query_key = grams[u][:BLOCK]
            key_key = jnp.where(strictly, grams[u][BLOCK:], 0.0)
            for h in range(heads):
                cum = jnp.broadcast_to(columns[u][:, h : h + 1], (BLOCK, BLOCK))
                gb = jnp.broadcast_to(columns[u][:, heads + h : heads + h + 1], (BLOCK, BLOCK))
                ratio = jnp.exp(jnp.where(lower, cum - tiles[u][h : h + 1], -1e30))
                stricts.append(ratio * key_key * gb)
                scores.append((ratio * query_key).astype(BF16))
                fades.append(jnp.exp(cum))
                gains.append(gb)
        inverses = unit_inverses(stricts)
        writes = []
        for u in blocks:
            for h in range(heads):
                n = u * heads + h
                scaled_k = (keys[u].astype(F32) * (gains[n] * fades[n])).astype(BF16)
                scaled_v = (values[u][h].astype(F32) * gains[n]).astype(BF16)
                both = jnp.concatenate([scaled_k, scaled_v], axis=1)
                writes.append(dot(inverses[n], both).astype(BF16))
        for u in blocks:
            for h in range(heads):
                n = u * heads + h
                cum_row = tiles[u][h : h + 1]
                last = cum_row[:, BLOCK - 1 : BLOCK]
                tails = (keys_t[u].astype(F32) * jnp.exp(last - cum_row)).astype(BF16)
                r = dot(jnp.concatenate([tails, scores[n]], axis=0), writes[n])
                at = (p * heads + h) * nblk + g * UNROLL + u
                aq[at, 0:DK, :] = (-r[:DK, :DK]).astype(BF16)
                binp[at] = r[:DK, DK:]
                aq[at, DK:, :] = (queries[u].astype(F32) * fades[n] - r[DK:, :DK]).astype(BF16)
                base_out[at] = r[DK:, DK:]
                gates[pl.ds(at, 1), :] = jnp.broadcast_to(jnp.exp(last), (1, BLOCK))
        return 0

    lax.fori_loop(0, nblk // UNROLL, group, 0)

    @pl.when(p == prompts - 1)
    def _():
        chains = carry.shape[0]
        for n in range(chains):
            at = n * nblk
            gate = gates[at : at + 1, :]
            carry[n, :, DK:] = binp[at]
            carry[n, :, :DK] = jnp.where(before == after, gate, 0.0) + aq[at, 0:DK, :].astype(F32)
            m_ref[n, 0:BLOCK, :] = aq[at, DK:, :]
            out_ref[n, 0:BLOCK, :] = base_out[at].astype(BF16)

        def step(c, _):
            for n in range(chains):
                at = n * nblk + c
                state = carry[n]
                r = dot(aq[at], state.astype(BF16))
                gate = gates[pl.ds(at, 1), :]
                carry[n, :, :DK] = gate * state[:, :DK] + r[:DK, :DK]
                carry[n, :, DK:] = gate * state[:, DK:] + r[:DK, DK:] + binp[at]
                tokens = pl.ds(pl.multiple_of(c * BLOCK, BLOCK), BLOCK)
                m_ref[n, tokens, :] = r[DK:, :DK].astype(BF16)
                out_ref[n, tokens, :] = (r[DK:, DK:] + base_out[at]).astype(BF16)
            return 0

        lax.fori_loop(1, nblk, step, 0)
        for n in range(chains):
            st_ref[n] = carry[n].astype(BF16)


def local_maps(first, lengths, qk, v, rim, conv_qk, conv_v, log_decay, write_gain):
    prompts, tok = v.shape[:2]
    heads = log_decay.shape[1]
    chains = prompts * heads
    nblk = tok // BLOCK
    units = chains * nblk

    def per_prompt(*shape):
        return pl.BlockSpec((1,) + shape, lambda p: (p,) + (0,) * len(shape))

    def whole(*shape):
        return pl.BlockSpec(shape, lambda p: (0,) * len(shape))

    smem = pl.BlockSpec(memory_space=pltpu.SMEM)
    return pl.pallas_call(
        maps_kernel,
        grid=(prompts,),
        in_specs=[
            smem,
            smem,
            per_prompt(2 * tok, DK),
            per_prompt(tok, heads * DV),
            per_prompt((1 + heads) * RIM, DK),
            whole(*conv_qk.shape),
            whole(*conv_v.shape),
            per_prompt(heads, tok),
            per_prompt(heads, tok),
        ],
        out_specs=[
            whole(chains, tok, DK),
            whole(chains, tok, DV),
            whole(chains, DK, DK + DV),
        ],
        out_shape=[
            jax.ShapeDtypeStruct((chains, tok, DK), BF16),
            jax.ShapeDtypeStruct((chains, tok, DV), BF16),
            jax.ShapeDtypeStruct((chains, DK, DK + DV), BF16),
        ],
        scratch_shapes=[
            pltpu.VMEM((RIM + 2 * tok, DK), F32),
            pltpu.VMEM((heads, RIM + tok, DV), F32),
            pltpu.VMEM((8 * nblk, BLOCK), F32),
            pltpu.VMEM((units, BLOCK), F32),
            pltpu.VMEM((units, 2 * BLOCK, DK), BF16),
            pltpu.VMEM((units, DK, DV), F32),
            pltpu.VMEM((units, BLOCK, DV), F32),
            pltpu.VMEM((chains, DK, DK + DV), F32),
        ],
        compiler_params=pltpu.CompilerParams(vmem_limit_bytes=VMEM_LIMIT),
        name="local_maps",
    )(first, lengths, qk, v, rim, conv_qk, conv_v, log_decay, write_gain)


def finish_kernel(first_ref, len_ref, maps_ref, m_ref, local_ref, z_ref, norm_ref, att_ref, final_ref):
    p = pl.program_id(0)
    count, heads = maps_ref.shape[:2]
    tok = z_ref.shape[1]
    mine = first_ref[0] // tok
    norm_gain = norm_ref[...]
    states = [jnp.zeros((DK, DV), F32) for _ in range(heads)]
    enters = [jnp.zeros((DK, DV), F32) for _ in range(heads)]
    for k in range(count):
        for h in range(heads):
            enters[h] = jnp.where(mine == k, states[h], enters[h])
            st = maps_ref[k, h]
            states[h] = dot(st[:, :DK], states[h].astype(BF16)) + st[:, DK:].astype(F32)
    for h in range(heads):
        final_ref[h] = states[h].astype(BF16)
    enters = [e.astype(BF16) for e in enters]
    step = 128

    def tokens(i, _):
        at = pl.ds(pl.multiple_of(i * step, step), step)
        position = first_ref[0] + i * step + lax.broadcasted_iota(jnp.int32, (step, DV), 0)
        valid = position < len_ref[p]
        for h in range(heads):
            raw = dot(m_ref[h, at, :], enters[h]) + local_ref[h, at, :].astype(F32)
            scaled = raw * lax.rsqrt(jnp.mean(raw * raw, axis=-1, keepdims=True) + EPSILON)
            z = z_ref[0, at, h * DV : (h + 1) * DV].astype(F32)
            gated = scaled * norm_gain * silu(z)
            att_ref[0, at, h * DV : (h + 1) * DV] = jnp.where(valid, gated, 0.0).astype(BF16)
        return 0

    lax.fori_loop(0, tok // step, tokens, 0, unroll=2)


def finish(first, lengths, maps, m, local, gate_z, norm_gain):
    prompts, tok, width = gate_z.shape
    heads = width // DV
    count = maps.shape[0]
    smem = pl.BlockSpec(memory_space=pltpu.SMEM)
    return pl.pallas_call(
        finish_kernel,
        grid=(prompts,),
        in_specs=[
            smem,
            smem,
            pl.BlockSpec((count, heads, DK, DK + DV), lambda p: (0, p, 0, 0)),
            pl.BlockSpec((heads, tok, DK), lambda p: (p, 0, 0)),
            pl.BlockSpec((heads, tok, DV), lambda p: (p, 0, 0)),
            pl.BlockSpec((1, tok, width), lambda p: (p, 0, 0)),
            pl.BlockSpec((1, DV), lambda p: (0, 0)),
        ],
        out_specs=[
            pl.BlockSpec((1, tok, width), lambda p: (p, 0, 0)),
            pl.BlockSpec((heads, DK, DV), lambda p: (p, 0, 0)),
        ],
        out_shape=[
            jax.ShapeDtypeStruct((prompts, tok, width), BF16),
            jax.ShapeDtypeStruct((prompts * heads, DK, DV), BF16),
        ],
        compiler_params=pltpu.CompilerParams(vmem_limit_bytes=VMEM_LIMIT),
        name="finish",
    )(first, lengths, maps, m, local, gate_z, norm_gain)


def shards(
    qk_in,
    v_in,
    gate_z,
    conv_qk,
    conv_v,
    log_decay,
    write_gain,
    norm_gain,
    prompt_lengths,
    placement,
):
    prompts, tok = v_in.shape[:2]
    heads = log_decay.shape[1]
    head_count = lax.axis_size("head")
    seq_count = lax.axis_size("seq")
    qk = qk_in.reshape(prompts, 2 * tok, DK)
    tails = jnp.concatenate(
        [qk[:, 2 * tok - RIM :]]
        + [v_in[:, tok - RIM :, h * DV : (h + 1) * DV] for h in range(heads)],
        axis=1,
    )
    rim = lax.ppermute(tails, "seq", [(i, i + 1) for i in range(seq_count - 1)])
    first = (lax.axis_index("seq") * tok).astype(jnp.int32).reshape(1)
    m, local, st = local_maps(
        first, prompt_lengths, qk, v_in, rim, conv_qk, conv_v, log_decay, write_gain
    )
    maps = lax.all_gather(st, "seq")
    attended, finals = finish(
        first, prompt_lengths, maps, m, local, gate_z, norm_gain.reshape(1, DV)
    )
    by_prompt = finals.reshape(prompts, heads, DK, DV)
    leaving = jnp.take(by_prompt, placement[0], axis=0)
    arrived = lax.all_to_all(leaving, "head", 0, 0, tiled=True)
    rollout = arrived.astype(F32).reshape(1, 1, head_count * heads, DK, DV)
    return attended, rollout


def solution(mesh):
    return jax.shard_map(
        shards,
        mesh=mesh,
        in_specs=(
            P(None, "seq", None, "head"),
            P(None, "seq", "head"),
            P(None, "seq", "head"),
            P(None, None, "head"),
            P(None, "head"),
            P(None, "head", "seq"),
            P(None, "head", "seq"),
            P(),
            P(),
            P("seq", None),
        ),
        out_specs=(P(None, "seq", "head"), P("seq", "head", None, None, None)),
        check_vma=False,
    )
```

profile of v0, /device:TPU:1, one launch (start us, length us, event | category | flops | bytes accessed | tf_op | source)
XLA Modules:
  0.0 125.9 jit_solution(14250399071337039946)
XLA Ops:
  7.2 0.0 all-gather.3.cloned.1.call-start
  7.2 0.7 fusion.1
  7.9 0.7 slice.14
  8.6 4.5 %collective-permute-start = (bf16[4,24,128]{2,1,0:T(8,128)(2,1)S(1)}, bf16[4,24,128]{2,1,0:T(8,128)(2,1)S(1)}, u32[]{:S(2)}, u32[]{:S(2)}) collective-permute-start(bf16[4,24,128]{2,1,0:T(8,128)(2,1)S(1)} %pad_maximum_fusion), channel_id=1, source_target_pairs={{0,16},{16,32},{32,48},{48,64},{64,80},{80,96},{96,112},{1,17},{17... | collective-permute-start | bytes 73736 | tf_op jit(solution)/shard_map/ppermute | solution.py:376
  13.1 0.9 collective-permute-done.rim_ref
  14.1 0.0 copy-start
  14.1 0.6 copy-done
  14.7 0.0 copy-start.1
  14.7 30.8 %local_maps.1 = (bf16[8,1024,128]{2,1,0:T(8,128)(2,1)}, bf16[8,1024,128]{2,1,0:T(8,128)(2,1)}, bf16[8,128,256]{2,1,0:T(8,128)(2,1)}) custom-call(s32[1]{0:T(128)} %bitcast.first_ref, s32[4]{0:T(128)} %len_ref.3, bf16[4,2048,128]{2,1,0:T(8,128)(2,1)} %bitcast.17, bf16[4,1024,256]{2,1,0:T(8,128)(2,1)} %v_ref.1, bf16[4,24,128]{2,1,0:T(8,128)(2,1)} %copy-done, ...), custom_call_target="tpu_custom_call" | custom-call | tf_op jit(solution)/shard_map/local_maps/pallas_call | solution.py:252
  45.4 0.0 all-gather.3.cloned.1.call-update
  45.5 0.0 copy-done.1
  45.5 35.5 %all-gather.3.cloned.1.call-done = bf16[64,128,256]{2,1,0:T(8,128)(2,1)} async-done(((bf16[8,128,256]{2,1,0:T(8,128)(2,1)}), bf16[64,128,256]{2,1,0:T(8,128)(2,1)}) %all-gather.3.cloned.1.call-update) | async-done | bytes 4194320 | tf_op jit(solution)/shard_map/all_gather | solution.py:381
  81.0 12.2 %finish.1 = (bf16[4,1024,256]{2,1,0:T(8,128)(2,1)}, bf16[8,128,128]{2,1,0:T(8,128)(2,1)}) custom-call(s32[1]{0:T(128)} %bitcast.first_ref, s32[4]{0:T(128)} %len_ref.3, bf16[8,8,128,256]{3,2,1,0:T(8,128)(2,1)} %bitcast.15, bf16[8,1024,128]{2,1,0:T(8,128)(2,1)} %get-tuple-element.8.m_ref, bf16[8,1024,128]{2,1,0:T(8,128)(2,1)} %get-tuple-element.9.local_ref, ...), custom_call_target="tpu_custom_call" | custom-call | tf_op jit(solution)/shard_map/finish/pallas_call | solution.py:329
  93.2 1.7 %gather_fusion = bf16[16,2,128,128]{3,2,1,0:T(8,128)(2,1)S(1)} fusion(bf16[4,2,128,128]{3,2,1,0:T(8,128)(2,1)} %bitcast.14, s32[1024]{0:T(1024)S(1)} %pad_clamp_fusion), kind=kCustom, calls=%fused_computation | custom fusion | bytes 2097216 | tf_op jit(solution)/shard_map/jit(_take)/gather | solution.py:386
  94.9 0.2 broadcast_select_fusion
  95.1 22.4 %all_to_all.5 = bf16[16,2,128,128]{3,2,1,0:T(8,128)(2,1)S(1)} all-to-all(bf16[16,2,128,128]{3,2,1,0:T(8,128)(2,1)S(1)} %broadcast_select_fusion), channel_id=1, replica_groups=mesh['seq'=8,'head'=16] {'head'}, dimensions={0} | all-to-all | bytes 2097152 | tf_op jit(solution)/shard_map/all_to_all | solution.py:387
  117.5 1.6 %convert.1 = f32[1,1,32,128,128]{4,3,2,1,0:T(8,128)} convert(bf16[1,1,32,128,128]{4,3,2,1,0:T(8,128)(2,1)S(1)} %bitcast.13) | non-fusion elementwise | flops 524288 | bytes 3145728 | tf_op jit(solution)/shard_map/reshape | solution.py:388
  (4 shorter events, 0.0 us)
Async XLA Ops:
  7.2 73.9 %all-gather.3.cloned.1.call-start = ((), (), s32[]{:S(2)}) async-start(), calls=%async_computation.1 | async-start | bytes 4718592 | tf_op jit(solution)/shard_map/all_gather | solution.py:381
  8.6 5.4 %collective-permute-start = (bf16[4,24,128]{2,1,0:T(8,128)(2,1)S(1)}, bf16[4,24,128]{2,1,0:T(8,128)(2,1)S(1)}, u32[]{:S(2)}, u32[]{:S(2)}) collective-permute-start(bf16[4,24,128]{2,1,0:T(8,128)(2,1)S(1)} %pad_maximum_fusion), channel_id=1, source_target_pairs={{0,16},{16,32},{32,48},{48,64},{64,80},{80,96},{96,112},{1,17},{17... | collective-permute-start | bytes 73736 | tf_op jit(solution)/shard_map/ppermute | solution.py:376
  14.1 0.6 copy-start
  14.7 30.8 %copy-start.1 = (s32[1,16]{1,0:T(1,128)S(1)}, s32[1,16]{1,0:T(1,128)}, u32[]{:S(2)}) copy-start(s32[1,16]{1,0:T(1,128)} %param.19) | copy-start | bytes 196
Sparse Core Ops, SparseCore 0:
  45.6 35.3 all-gather.2
where the time goes:
time: 127 us; the launch traced here: 126 us
  Pallas kernels  42.9 us (34%)
  waiting for transfers between devices  36.4 us (29%)
  blocking collectives  22.4 us (18%)
  between operations  14.1 us (11%)
  starting transfers between devices  4.53 us (4%)
  local copies, waits for them, and re-layouts  3.72 us (3%)
  other arithmetic  1.75 us (1%)
    all_gather x1, waiting for transfers between devices, shards(): maps = lax.all_gather(st, 'seq')  35.5 us
    pallas_call x1, Pallas kernels, local_maps(): pl.pallas_call(maps_kernel, grid=(prompts,), in_specs=[smem, smem, per_pr...  30.8 us
    all_to_all x1, blocking collectives, shards(): arrived = lax.all_to_all(leaving, 'head', 0, 0, tiled=True)  22.4 us
    pallas_call x1, Pallas kernels, finish(): pl.pallas_call(finish_kernel, grid=(prompts,), in_specs=[smem, smem, pl.B...  12.2 us
    ppermute x1, starting transfers between devices, shards(): rim = lax.ppermute(tails, 'seq', [(i, i + 1) for i in range(seq_count - 1)])  4.5 us
  transfers between devices with their start and end apart: 2, of which 2 were waited for; matrix products, arithmetic and copies ran while one was open for 0% of the time, Pallas kernels for 0%

commit v1 on v0

--- a/solution.py
+++ b/solution.py
@@ -232,7 +232,7 @@
 
         lax.fori_loop(1, nblk, step, 0)
         for n in range(chains):
-            st_ref[n] = carry[n].astype(BF16)
+            st_ref[n % heads, n // heads] = carry[n].astype(BF16)
 
 
 def local_maps(first, lengths, qk, v, rim, conv_qk, conv_v, log_decay, write_gain):
@@ -266,12 +266,12 @@
         out_specs=[
             whole(chains, tok, DK),
             whole(chains, tok, DV),
-            whole(chains, DK, DK + DV),
+            whole(heads, prompts, DK, DK + DV),
         ],
         out_shape=[
             jax.ShapeDtypeStruct((chains, tok, DK), BF16),
             jax.ShapeDtypeStruct((chains, tok, DV), BF16),
-            jax.ShapeDtypeStruct((chains, DK, DK + DV), BF16),
+            jax.ShapeDtypeStruct((heads, prompts, DK, DK + DV), BF16),
         ],
         scratch_shapes=[
             pltpu.VMEM((RIM + 2 * tok, DK), F32),
@@ -288,67 +288,245 @@
     )(first, lengths, qk, v, rim, conv_qk, conv_v, log_decay, write_gain)
 
 
-def finish_kernel(first_ref, len_ref, maps_ref, m_ref, local_ref, z_ref, norm_ref, att_ref, final_ref):
-    p = pl.program_id(0)
-    count, heads = maps_ref.shape[:2]
-    tok = z_ref.shape[1]
-    mine = first_ref[0] // tok
+def deliver_kernel(
+    len_ref,
+    place_ref,
+    maps_hbm,
+    m_hbm,
+    local_hbm,
+    z_hbm,
+    norm_ref,
+    att_hbm,
+    roll_hbm,
+    maps,
+    m,
+    local,
+    z,
+    att,
+    pair,
+    gathered,
+    back,
+    got,
+    enters,
+    finals,
+    leaving,
+    load_sem,
+    store_sem,
+    pair_send,
+    pair_recv,
+    x_send,
+    x_recv,
+    back_send,
+    back_recv,
+    head_send,
+    head_recv,
+    own_sem,
+):
+    heads, prompts = maps.shape[:2]
+    tok = z.shape[1]
+    chips = gathered.shape[1]
+    s = lax.axis_index("seq")
+    row = lax.axis_index("head")
+    rows_count = leaving.shape[0]
+    core = lax.rem(s, 2)
+    chip = lax.div(s, 2)
+    mesh_id = pl.DeviceIdType.MESH
+    partner = (chip * 2 + 1 - core, row)
+
+    def along_x(d):
+        return (lax.rem(chip + d, chips) * 2 + core, row)
+
+    def in_row(d):
+        return lax.rem(row + d, rows_count)
+
+    loads = [
+        pltpu.make_async_copy(src, dst, load_sem.at[i])
+        for i, (src, dst) in enumerate(
+            [(maps_hbm, maps), (m_hbm, m), (local_hbm, local), (z_hbm, z)]
+        )
+    ]
+    for load in loads:
+        load.start()
+    barrier = pltpu.get_barrier_semaphore()
+    peers = [partner] + [along_x(d) for d in range(1, chips)]
+    peers += [(s, in_row(d)) for d in range(1, rows_count)]
+    for peer in peers:
+        pl.semaphore_signal(barrier, inc=1, device_id=peer, device_id_type=mesh_id)
+    pl.semaphore_wait(barrier, len(peers))
+
+    loads[0].wait()
+    swaps = []
+    for p in range(prompts):
+        swap = pltpu.make_async_remote_copy(
+            maps.at[1 - core, p],
+            pair.at[p],
+            pair_send.at[p],
+            pair_recv.at[p],
+            device_id=partner,
+            device_id_type=mesh_id,
+        )
+        swap.start()
+        swaps.append(swap)
+    spreads = []
+    for p in range(prompts):
+        swaps[p].wait_recv()
+        own = maps[core, p]
+        other = pair[p]
+        early = jnp.where(core == 0, own, other)
+        late = jnp.where(core == 0, other, own)
+        both = dot(late[:, :DK], early)
+        joined = jnp.concatenate(
+            [both[:, :DK], both[:, DK:] + late[:, DK:].astype(F32)], axis=1
+        )
+        gathered[p, chip] = joined.astype(BF16)
+        for d in range(1, chips):
+            spread = pltpu.make_async_remote_copy(
+                gathered.at[p, chip],
+                gathered.at[p, chip],
+                x_send.at[p, d - 1],
+                x_recv.at[p, d - 1],
+                device_id=along_x(d),
+                device_id_type=mesh_id,
+            )
+            spread.start()
+            spreads.append(spread)
+    returns = []
+    for p in range(prompts):
+        for d in range(1, chips):
+            spreads[p * (chips - 1) + d - 1].wait_recv()
+        state = jnp.zeros((DK, DV), F32)
+        enter = state
+        for k in range(chips):
+            enter = jnp.where(chip == k, state, enter)
+            tk = gathered[p, k]
+            if k == 0:
+                state = tk[:, DK:].astype(F32)
+            else:
+                state = dot(tk[:, :DK], state.astype(BF16)) + tk[:, DK:].astype(F32)
+        first_map = jnp.where(core == 0, maps[core, p], pair[p])
+        enter = enter.astype(BF16)
+        second = (dot(first_map[:, :DK], enter) + first_map[:, DK:].astype(F32)).astype(BF16)
+        final = state.astype(BF16)
+        finals[core, p] = final
+        enters[core, p] = jnp.where(core == 0, enter, second)
+        back[p, 0] = jnp.where(core == 0, second, enter)
+        back[p, 1] = final
+        ret = pltpu.make_async_remote_copy(
+            back.at[p],
+            got.at[p],
+            back_send.at[p],
+            back_recv.at[p],
+            device_id=partner,
+            device_id_type=mesh_id,
+        )
+        ret.start()
+        returns.append(ret)
+    for p in range(prompts):
+        returns[p].wait_recv()
+        enters[1 - core, p] = got[p, 0]
+        finals[1 - core, p] = got[p, 1]
+    sends = []
+    for d in range(1, rows_count):
+        to = in_row(d)
+        chosen = place_ref[0, to]
+        for h in range(heads):
+            leaving[d, h] = finals[h, chosen]
+        send = pltpu.make_async_remote_copy(
+            leaving.at[d],
+            roll_hbm.at[row],
+            head_send.at[d],
+            head_recv.at[d],
+            device_id=(s, to),
+            device_id_type=mesh_id,
+        )
+        send.start()
+        sends.append(send)
+    chosen = place_ref[0, row]
+    for h in range(heads):
+        leaving[0, h] = finals[h, chosen]
+    keep = pltpu.make_async_copy(leaving.at[0], roll_hbm.at[row], own_sem)
+    keep.start()
+
+    for load in loads[1:]:
+        load.wait()
     norm_gain = norm_ref[...]
-    states = [jnp.zeros((DK, DV), F32) for _ in range(heads)]
-    enters = [jnp.zeros((DK, DV), F32) for _ in range(heads)]
-    for k in range(count):
-        for h in range(heads):
-            enters[h] = jnp.where(mine == k, states[h], enters[h])
-            st = maps_ref[k, h]
-            states[h] = dot(st[:, :DK], states[h].astype(BF16)) + st[:, DK:].astype(F32)
-    for h in range(heads):
-        final_ref[h] = states[h].astype(BF16)
-    enters = [e.astype(BF16) for e in enters]
     step = 128
 
-    def tokens(i, _):
-        at = pl.ds(pl.multiple_of(i * step, step), step)
-        position = first_ref[0] + i * step + lax.broadcasted_iota(jnp.int32, (step, DV), 0)
-        valid = position < len_ref[p]
-        for h in range(heads):
-            raw = dot(m_ref[h, at, :], enters[h]) + local_ref[h, at, :].astype(F32)
-            scaled = raw * lax.rsqrt(jnp.mean(raw * raw, axis=-1, keepdims=True) + EPSILON)
-            z = z_ref[0, at, h * DV : (h + 1) * DV].astype(F32)
-            gated = scaled * norm_gain * silu(z)
-            att_ref[0, at, h * DV : (h + 1) * DV] = jnp.where(valid, gated, 0.0).astype(BF16)
+    def prompt(p, _):
+        length = len_ref[p]
+
+        def tokens(i, _):
+            at = pl.ds(pl.multiple_of(i * step, step), step)
+            position = s * tok + i * step + lax.broadcasted_iota(jnp.int32, (step, DV), 0)
+            valid = position < length
+            for h in range(heads):
+                n = p * heads + h
+                raw = dot(m[n, at, :], enters[h, p]) + local[n, at, :].astype(F32)
+                scaled = raw * lax.rsqrt(jnp.mean(raw * raw, axis=-1, keepdims=True) + EPSILON)
+                zh = z[p, at, h * DV : (h + 1) * DV].astype(F32)
+                gated = scaled * norm_gain * silu(zh)
+                att[p, at, h * DV : (h + 1) * DV] = jnp.where(valid, gated, 0.0).astype(BF16)
+            return 0
+
+        lax.fori_loop(0, tok // step, tokens, 0, unroll=2)
         return 0
 
-    lax.fori_loop(0, tok // step, tokens, 0, unroll=2)
-
-
-def finish(first, lengths, maps, m, local, gate_z, norm_gain):
+    lax.fori_loop(0, prompts, prompt, 0)
+    store = pltpu.make_async_copy(att, att_hbm, store_sem)
+    store.start()
+    for copy in swaps + spreads + returns:
+        copy.wait_send()
+    for send in sends:
+        send.wait()
+    keep.wait()
+    store.wait()
+
+
+def deliver(lengths, placement, maps, m, local, gate_z, norm_gain, chips, rows_count):
     prompts, tok, width = gate_z.shape
-    heads = width // DV
-    count = maps.shape[0]
+    heads = maps.shape[0]
     smem = pl.BlockSpec(memory_space=pltpu.SMEM)
+    hbm = pl.BlockSpec(memory_space=pl.ANY)
+    vmem = pl.BlockSpec(memory_space=pltpu.VMEM)
+    dma = pltpu.SemaphoreType.DMA
     return pl.pallas_call(
-        finish_kernel,
-        grid=(prompts,),
-        in_specs=[
-            smem,
-            smem,
-            pl.BlockSpec((count, heads, DK, DK + DV), lambda p: (0, p, 0, 0)),
-            pl.BlockSpec((heads, tok, DK), lambda p: (p, 0, 0)),
-            pl.BlockSpec((heads, tok, DV), lambda p: (p, 0, 0)),
-            pl.BlockSpec((1, tok, width), lambda p: (p, 0, 0)),
-            pl.BlockSpec((1, DV), lambda p: (0, 0)),
-        ],
-        out_specs=[
-            pl.BlockSpec((1, tok, width), lambda p: (p, 0, 0)),
-            pl.BlockSpec((heads, DK, DV), lambda p: (p, 0, 0)),
-        ],
+        deliver_kernel,
+        in_specs=[smem, smem, hbm, hbm, hbm, hbm, vmem],
+        out_specs=[hbm, hbm],
         out_shape=[
             jax.ShapeDtypeStruct((prompts, tok, width), BF16),
-            jax.ShapeDtypeStruct((prompts * heads, DK, DV), BF16),
+            jax.ShapeDtypeStruct((rows_count, heads, DK, DV), BF16),
         ],
-        compiler_params=pltpu.CompilerParams(vmem_limit_bytes=VMEM_LIMIT),
-        name="finish",
-    )(first, lengths, maps, m, local, gate_z, norm_gain)
+        scratch_shapes=[
+            pltpu.VMEM(maps.shape, BF16),
+            pltpu.VMEM(m.shape, BF16),
+            pltpu.VMEM(local.shape, BF16),
+            pltpu.VMEM(gate_z.shape, BF16),
+            pltpu.VMEM(gate_z.shape, BF16),
+            pltpu.VMEM((prompts, DK, DK + DV), BF16),
+            pltpu.VMEM((prompts, chips, DK, DK + DV), BF16),
+            pltpu.VMEM((prompts, 2, DK, DV), BF16),
+            pltpu.VMEM((prompts, 2, DK, DV), BF16),
+            pltpu.VMEM((heads, prompts, DK, DV), BF16),
+            pltpu.VMEM((heads, prompts, DK, DV), BF16),
+            pltpu.VMEM((rows_count, heads, DK, DV), BF16),
+            dma((4,)),
+            dma,
+            dma((prompts,)),
+            dma((prompts,)),
+            dma((prompts, chips - 1)),
+            dma((prompts, chips - 1)),
+            dma((prompts,)),
+            dma((prompts,)),
+            dma((rows_count,)),
+            dma((rows_count,)),
+            dma,
+        ],
+        compiler_params=pltpu.CompilerParams(
+            vmem_limit_bytes=VMEM_LIMIT, collective_id=0, has_side_effects=True
+        ),
+        name="deliver",
+    )(lengths, placement, maps, m, local, gate_z, norm_gain)
 
 
 def shards(
@@ -378,13 +556,17 @@
     m, local, st = local_maps(
         first, prompt_lengths, qk, v_in, rim, conv_qk, conv_v, log_decay, write_gain
     )
-    maps = lax.all_gather(st, "seq")
-    attended, finals = finish(
-        first, prompt_lengths, maps, m, local, gate_z, norm_gain.reshape(1, DV)
+    attended, arrived = deliver(
+        prompt_lengths,
+        placement,
+        st,
+        m,
+        local,
+        gate_z,
+        norm_gain.reshape(1, DV),
+        seq_count // 2,
+        head_count,
     )
-    by_prompt = finals.reshape(prompts, heads, DK, DV)
-    leaving = jnp.take(by_prompt, placement[0], axis=0)
-    arrived = lax.all_to_all(leaving, "head", 0, 0, tiled=True)
     rollout = arrived.astype(F32).reshape(1, 1, head_count * heads, DK, DV)
     return attended, rollout
 

time: 127 us -> 84.4 us (0.66)
  waiting for transfers between devices: 36.4 us -> 0.92 us
  Pallas kernels: 42.9 us -> 71 us
  blocking collectives: 22.4 us -> 0 us
  between operations: 14.1 us -> 0.66 us
    all_gather x1 -> x0, waiting for transfers between devices: 35.5 us -> none  [shards(): maps = lax.all_gather(st, 'seq')]
    pallas_call x1, Pallas kernels: 12.2 us -> 40.3 us  [deliver(): pl.pallas_call(deliver_kernel, in_specs=[smem, smem, hbm, hbm, hbm, hbm,...]
    all_to_all x1 -> x0, blocking collectives: 22.4 us -> none  [shards(): arrived = lax.all_to_all(leaving, 'head', 0, 0, tiled=True)]
    gather x1 -> x0, local copies, waits for them, and re-layouts: 1.7 us -> none  [shards(): leaving = jnp.take(by_prompt, placement[0], axis=0)]
    reshape x1, other arithmetic: 1.56 us -> 2.94 us  [shards(): rollout = arrived.astype(F32).reshape(1, 1, head_count * heads, DK, DV)]
    unnamed x4 -> x5, local copies, waits for them, and re-layouts: 0.61 us -> 1.93 us
  transfers between devices with their start and end apart: 2 -> 1, of which waited for: 2 -> 1; matrix products, arithmetic and copies ran while one was open for 0% -> 0% of each run, Pallas kernels for 0% -> 0%
where the time goes in v1:
time: 84.4 us; the launch traced here: 83.4 us
  Pallas kernels  71 us (84%)
  starting transfers between devices  4.5 us (5%)
  local copies, waits for them, and re-layouts  3.34 us (4%)
  other arithmetic  2.94 us (3%)
  waiting for transfers between devices  0.92 us (1%)
    pallas_call x1, Pallas kernels, deliver(): pl.pallas_call(deliver_kernel, in_specs=[smem, smem, hbm, hbm, hbm, hbm,...  40.3 us
    pallas_call x1, Pallas kernels, local_maps(): pl.pallas_call(maps_kernel, grid=(prompts,), in_specs=[smem, smem, per_pr...  30.8 us
    ppermute x1, starting transfers between devices, shards(): rim = lax.ppermute(tails, 'seq', [(i, i + 1) for i in range(seq_count - 1)])  4.5 us
    reshape x1, other arithmetic, shards(): rollout = arrived.astype(F32).reshape(1, 1, head_count * heads, DK, DV)  2.94 us
    unnamed x5, local copies, waits for them, and re-layouts  1.93 us
  transfers between devices with their start and end apart: 1, of which 1 were waited for; matrix products, arithmetic and copies ran while one was open for 0% of the time, Pallas kernels for 0%

profile of v1, /device:TPU:1, one launch (start us, length us, event | category | flops | bytes accessed | tf_op | source)
XLA Modules:
  0.0 83.4 jit_solution(6229114572479408364)
XLA Ops:
  0.6 0.7 slice.12
  1.3 0.7 fusion
  2.1 4.5 %collective-permute-start = (bf16[4,24,128]{2,1,0:T(8,128)(2,1)S(1)}, bf16[4,24,128]{2,1,0:T(8,128)(2,1)S(1)}, u32[]{:S(2)}, u32[]{:S(2)}) collective-permute-start(bf16[4,24,128]{2,1,0:T(8,128)(2,1)S(1)} %pad_maximum_fusion), channel_id=1, source_target_pairs={{0,16},{16,32},{32,48},{48,64},{64,80},{80,96},{96,112},{1,17},{17... | collective-permute-start | bytes 73736 | tf_op jit(solution)/shard_map/ppermute | solution.py:554
  6.6 0.9 %collective-permute-done.rim_ref = bf16[4,24,128]{2,1,0:T(8,128)(2,1)S(1)} collective-permute-done((bf16[4,24,128]{2,1,0:T(8,128)(2,1)S(1)}, bf16[4,24,128]{2,1,0:T(8,128)(2,1)S(1)}, u32[]{:S(2)}, u32[]{:S(2)}) %collective-permute-start) | collective-permute-done | bytes 24608 | tf_op jit(solution)/shard_map/ppermute | solution.py:554
  7.5 0.0 copy-start.1
  7.5 0.6 copy-done.1
  8.1 30.8 %local_maps.1 = (bf16[8,1024,128]{2,1,0:T(8,128)(2,1)}, bf16[8,1024,128]{2,1,0:T(8,128)(2,1)}, bf16[2,4,128,256]{3,2,1,0:T(8,128)(2,1)}) custom-call(s32[1]{0:T(128)} %bitcast.first_ref, s32[4]{0:T(128)} %len_ref.3, bf16[4,2048,128]{2,1,0:T(8,128)(2,1)} %bitcast.6, bf16[4,1024,256]{2,1,0:T(8,128)(2,1)} %v_ref.1, bf16[4,24,128]{2,1,0:T(8,128)(2,1)} %copy-done.1, ...), custom_call_target="tpu_custom_call" | custom-call | tf_op jit(solution)/shard_map/local_maps/pallas_call | solution.py:252
  38.8 40.3 %deliver.1 = (bf16[4,1024,256]{2,1,0:T(8,128)(2,1)}, bf16[16,2,128,128]{3,2,1,0:T(8,128)(2,1)}) custom-call(s32[4]{0:T(128)} %len_ref.3, s32[1,16]{1,0:T(1,128)} %place_ref.1, bf16[2,4,128,256]{3,2,1,0:T(8,128)(2,1)} %get-tuple-element.7.maps_hbm, bf16[8,1024,128]{2,1,0:T(8,128)(2,1)} %get-tuple-element.8.m_hbm, ...), custom_call_target="tpu_custom_call" | custom-call | tf_op jit(solution)/shard_map/deliver/pallas_call | solution.py:492
  79.1 0.0 copy-start
  79.1 2.9 %convert.1 = f32[1,1,32,128,128]{4,3,2,1,0:T(8,128)} convert(bf16[1,1,32,128,128]{4,3,2,1,0:T(8,128)(2,1)} %bitcast.7) | non-fusion elementwise | flops 524288 | bytes 3145728 | tf_op jit(solution)/shard_map/reshape | solution.py:570
  82.1 0.0 copy-done
  82.1 1.3 %copy.13 = bf16[4,1024,256]{2,1,0:T(8,128)(2,1)} copy(bf16[4,1024,256]{2,1,0:T(8,128)(2,1)S(1)} %copy-done) | data formatting | bytes 4194304
  (1 shorter events, 0.0 us)
Async XLA Ops:
  2.1 5.4 %collective-permute-start = (bf16[4,24,128]{2,1,0:T(8,128)(2,1)S(1)}, bf16[4,24,128]{2,1,0:T(8,128)(2,1)S(1)}, u32[]{:S(2)}, u32[]{:S(2)}) collective-permute-start(bf16[4,24,128]{2,1,0:T(8,128)(2,1)S(1)} %pad_maximum_fusion), channel_id=1, source_target_pairs={{0,16},{16,32},{32,48},{48,64},{64,80},{80,96},{96,112},{1,17},{17... | collective-permute-start | bytes 73736 | tf_op jit(solution)/shard_map/ppermute | solution.py:554
  7.5 0.6 copy-start.1
  79.1 3.0 %copy-start = (bf16[4,1024,256]{2,1,0:T(8,128)(2,1)S(1)}, bf16[4,1024,256]{2,1,0:T(8,128)(2,1)}, u32[]{:S(2)}) copy-start(bf16[4,1024,256]{2,1,0:T(8,128)(2,1)} %get-tuple-element.16) | copy-start | bytes 6291460

commit v2 on v0

v2 whole, which is shorter than its diff:
```python
import functools

import jax
import jax.numpy as jnp
from jax import lax
from jax.experimental import pallas as pl
from jax.experimental.pallas import tpu as pltpu
from jax.sharding import PartitionSpec as P

DK = 128
DV = 128
CONV = 4
BLOCK = 128
BASE = 16
UNROLL = 4
RIM = 16
EPSILON = 1e-06
F32 = jnp.float32
BF16 = jnp.bfloat16
VMEM_LIMIT = 56 * 1024 * 1024


def dot(a, b):
    return jnp.dot(a, b, preferred_element_type=F32)


def silu(x):
    half = 0.5 * x
    return half + half * jnp.tanh(half)


def base_inverses(stricts):
    half = BASE // 2
    lane = lax.broadcasted_iota(jnp.int32, (half, BLOCK), 1)
    row = lax.broadcasted_iota(jnp.int32, (half, BLOCK), 0)
    home = lane // BASE
    tops, bots, lows_top, lows_bot = [], [], [], []
    for s in stricts:
        top, bot = s[0:half], s[half:BASE]
        for b in range(1, BLOCK // BASE):
            top = jnp.where(home == b, s[b * BASE : b * BASE + half], top)
            bot = jnp.where(home == b, s[b * BASE + half : (b + 1) * BASE], bot)
        lows_top.append(top)
        lows_bot.append(bot)
        tops.append(jnp.where(lane % BASE == row, 1.0, 0.0).astype(F32))
        bots.append(jnp.where(lane % BASE == row + half, 1.0, 0.0).astype(F32))
    for j in range(BASE - 1):
        index = home * BASE + j
        for n in range(len(stricts)):
            source = tops[n][j : j + 1] if j < half else bots[n][j - half : j - half + 1]
            if j < half - 1:
                tops[n] = tops[n] - jnp.take_along_axis(lows_top[n], index, axis=1) * source
            bots[n] = bots[n] - jnp.take_along_axis(lows_bot[n], index, axis=1) * source
    return [jnp.concatenate([t, b], axis=0) for t, b in zip(tops, bots)]


def merge_levels(slabs, lows):
    size = BASE
    while size < BLOCK // 2:
        per = size // BASE
        lane_slab = lax.broadcasted_iota(jnp.int32, (size, BLOCK), 1) // size
        odd = [o for o in range(1, BLOCK // size, 2)]
        lefts = [
            jnp.concatenate([slab for o in odd for slab in sl[o * per : (o + 1) * per]], axis=0)
            for sl in slabs
        ]
        wholes = [jnp.concatenate(sl, axis=0) for sl in slabs]
        keep = jnp.concatenate([(lane_slab == o - 1).astype(F32) for o in odd], axis=0) > 0.5
        ys = [jnp.where(keep, dot(a, low), 0.0).astype(BF16) for a, low in zip(lefts, lows)]
        zs = [dot(y, w) for y, w in zip(ys, wholes)]
        for n, z in enumerate(zs):
            new = (lefts[n].astype(F32) - z).astype(BF16)
            for m, o in enumerate(odd):
                for i in range(per):
                    at = m * size + i * BASE
                    slabs[n][o * per + i] = new[at : at + BASE]
        size *= 2


def delta_kernel(
    len_ref,
    place_ref,
    qk_hbm,
    v_hbm,
    z_hbm,
    cqk_ref,
    cv_ref,
    ld_ref,
    wg_ref,
    norm_ref,
    att_hbm,
    roll_hbm,
    qk,
    v,
    z,
    att,
    rim_qk,
    rim_v,
    xqk,
    xv,
    rows,
    m,
    local,
    carry,
    strict_a,
    strict_b,
    base_a,
    base_b,
    left_a,
    left_b,
    both_a,
    both_b,
    fadeq_a,
    fadeq_b,
    gate_a,
    gate_b,
    aq_0,
    aq_1,
    binp_0,
    binp_1,
    bout_0,
    bout_1,
    step_0,
    step_1,
    maps,
    pair,
    gathered,
    back,
    got,
    enters,
    finals,
    leaving,
    qk_sem,
    v_sem,
    z_sem,
    store_sem,
    rim_send,
    rim_recv,
    pair_send,
    pair_recv,
    x_send,
    x_recv,
    back_send,
    back_recv,
    head_send,
    head_recv,
    own_sem,
):
    prompts, tok = v.shape[:2]
    heads = ld_ref.shape[1]
    nblk = tok // BLOCK
    half_tok = UNROLL * BLOCK
    chips = gathered.shape[1]
    rows_count = leaving.shape[0]
    seq_count = 2 * chips
    s = lax.axis_index("seq")
    row = lax.axis_index("head")
    core = lax.rem(s, 2)
    chip = lax.div(s, 2)
    mesh_id = pl.DeviceIdType.MESH
    partner = (chip * 2 + 1 - core, row)
    following = (lax.rem(s + 1, seq_count), row)
    preceding = (lax.rem(s + seq_count - 1, seq_count), row)
    sets = {
        1: (strict_b, base_b, left_b, both_b, fadeq_b, gate_b),
        0: (strict_a, base_a, left_a, both_a, fadeq_a, gate_a),
    }

    def results(p, half):
        if half == 0:
            return aq_0, binp_0, bout_0, step_0
        return [ref.at[lax.rem(p, 2)] for ref in (aq_1, binp_1, bout_1, step_1)]

    def along_x(d):
        return (lax.rem(chip + d, chips) * 2 + core, row)

    def in_row(d):
        return lax.rem(row + d, rows_count)

    def load_qk(p):
        return pltpu.make_async_copy(qk_hbm.at[p], qk.at[p], qk_sem.at[p])

    def load_v(p):
        return pltpu.make_async_copy(v_hbm.at[p], v.at[p], v_sem.at[p])

    load_z = pltpu.make_async_copy(z_hbm, z, z_sem)
    for p in range(prompts):
        load_qk(p).start()
        load_v(p).start()
    load_z.start()
    barrier = pltpu.get_barrier_semaphore()
    peers = [following, preceding]
    peers += [along_x(d) for d in range(1, chips)]
    peers += [(s, in_row(d)) for d in range(1, rows_count)]
    for peer in peers:
        pl.semaphore_signal(barrier, inc=1, device_id=peer, device_id_type=mesh_id)

    before = lax.broadcasted_iota(jnp.int32, (BLOCK, BLOCK), 0)
    after = lax.broadcasted_iota(jnp.int32, (BLOCK, BLOCK), 1)
    lower = before >= after
    strictly = before > after
    upto = jnp.where(before <= after, 1.0, 0.0).astype(F32)
    rows[...] = jnp.zeros_like(rows)
    position = lax.broadcasted_iota(jnp.int32, (heads, tok), 1) + s * tok
    for p in range(prompts):
        valid = position < len_ref[p]
        log_gate = jnp.where(valid, ld_ref[p], 0.0)
        gain = jnp.where(valid, wg_ref[p], 0.0)
        for c in range(nblk):
            at = 8 * (p * nblk + c)
            rows[at : at + heads, :] = log_gate[:, c * BLOCK : (c + 1) * BLOCK]
            rows[at + heads : at + 2 * heads, :] = gain[:, c * BLOCK : (c + 1) * BLOCK]
    raw_rows = rows[...]
    sums = jnp.dot(raw_rows, upto, precision=lax.Precision.HIGHEST, preferred_element_type=F32)
    kind = lax.broadcasted_iota(jnp.int32, raw_rows.shape, 0) % 8
    rows[...] = jnp.where(kind < heads, sums, raw_rows)
    taps_qk = cqk_ref[...].astype(F32)
    taps_v = cv_ref[...].astype(F32)

    def prepare(p, half):
        strict_ref, base_ref, left_ref, both_ref, fadeq_ref, gate_ref = sets[half]
        blocks = range(UNROLL)
        start = half * half_tok
        if half == 0:
            scale = jnp.where(s == 0, 0.0, 1.0).astype(F32)
            xqk[0:RIM, :] = rim_qk[p].astype(F32) * scale
        else:
            xqk[0:RIM, :] = qk[p, 2 * start - RIM : 2 * start, :].astype(F32)
        xqk[RIM:, :] = qk[p, 2 * start : 2 * (start + half_tok), :].astype(F32)
        for h in range(heads):
            lanes = slice(h * DV, (h + 1) * DV)
            if half == 0:
                xv[h, 0:RIM, :] = rim_v[p, :, lanes].astype(F32) * scale
            else:
                xv[h, 0:RIM, :] = v[p, start - RIM : start, lanes].astype(F32)
            xv[h, RIM:, :] = v[p, start : start + half_tok, lanes].astype(F32)

        def mixed(u, which):
            total = None
            for i in range(CONV):
                at = RIM + 2 * (u * BLOCK - (CONV - 1) + i) + which
                term = xqk[pl.ds(at, BLOCK, stride=2), :] * taps_qk[i, which : which + 1, :]
                total = term if total is None else total + term
            return silu(total)

        def unit(x):
            return x * lax.rsqrt(jnp.sum(x * x, axis=-1, keepdims=True) + EPSILON)

        queries, keys, keys_t, values, tiles, columns = [], [], [], [], [], []
        for u in blocks:
            q = unit(mixed(u, 0))
            k = unit(mixed(u, 1))
            queries.append(q.astype(BF16))
            keys.append(k.astype(BF16))
            keys_t.append(k.T.astype(BF16))
            vs = []
            for h in range(heads):
                total = None
                for i in range(CONV):
                    at = RIM + u * BLOCK - (CONV - 1) + i
                    term = xv[h, at : at + BLOCK, :] * taps_v[i : i + 1, h * DV : (h + 1) * DV]
                    total = term if total is None else total + term
                vs.append(silu(total).astype(BF16))
            values.append(vs)
            at = pl.multiple_of(8 * (p * nblk + half * UNROLL + u), 8)
            tile = rows[pl.ds(at, 8), :]
            tiles.append(tile)
            columns.append(tile.T)
        grams = [dot(jnp.concatenate([queries[u], keys[u]], axis=0), keys_t[u]) for u in blocks]
        stricts = []
        for u in blocks:
            query_key = grams[u][:BLOCK]
            key_key = jnp.where(strictly, grams[u][BLOCK:], 0.0)
            for h in range(heads):
                n = u * heads + h
                cum_row = tiles[u][h : h + 1]
                last = cum_row[:, BLOCK - 1 : BLOCK]
                cum = jnp.broadcast_to(columns[u][:, h : h + 1], (BLOCK, BLOCK))
                gb = jnp.broadcast_to(columns[u][:, heads + h : heads + h + 1], (BLOCK, BLOCK))
                ratio = jnp.exp(jnp.where(lower, cum - cum_row, -1e30))
                fade = jnp.exp(cum)
                strict = ratio * key_key * gb
                stricts.append(strict)
                strict_ref[n] = strict.astype(BF16)
                left_ref[n, 0:DK, :] = (
                    keys_t[u].astype(F32) * jnp.exp(last - cum_row)
                ).astype(BF16)
                left_ref[n, DK:, :] = (ratio * query_key).astype(BF16)
                both_ref[n, :, 0:DK] = (keys[u].astype(F32) * (gb * fade)).astype(BF16)
                both_ref[n, :, DK:] = (values[u][h].astype(F32) * gb).astype(BF16)
                fadeq_ref[n] = queries[u].astype(F32) * fade
                gate_ref[n : n + 1, :] = jnp.broadcast_to(jnp.exp(last), (1, BLOCK))
        for n, x in enumerate(base_inverses(stricts)):
            base_ref[n] = x

    def solve(p, half):
        strict_ref, base_ref, left_ref, both_ref, fadeq_ref, gate_ref = sets[half]
        aq, binp, bout, step = results(p, half)
        units = range(UNROLL * heads)
        mid = BLOCK // 2
        home = lax.broadcasted_iota(jnp.int32, (BASE, BLOCK), 1) // BASE
        lows = [strict_ref[n] for n in units]
        slabs = []
        for n in units:
            x = base_ref[n]
            slabs.append(
                [jnp.where(home == b, x, 0.0).astype(BF16) for b in range(BLOCK // BASE)]
            )
        merge_levels(slabs, lows)
        per = mid // BASE
        tops = [jnp.concatenate(sl[:per], axis=0)[:, :mid] for sl in slabs]
        bots = [jnp.concatenate(sl[per:], axis=0)[:, mid:] for sl in slabs]
        w1 = [dot(tops[n], both_ref[n, 0:mid, :]).astype(BF16) for n in units]
        rest = [
            (both_ref[n, mid:, :].astype(F32) - dot(lows[n][mid:, :mid], w1[n])).astype(BF16)
            for n in units
        ]
        w2 = [dot(bots[n], rest[n]).astype(BF16) for n in units]
        for n in units:
            r = dot(left_ref[n], jnp.concatenate([w1[n], w2[n]], axis=0))
            aq[n, 0:DK, :] = (-r[:DK, :DK]).astype(BF16)
            binp[n] = r[:DK, DK:]
            aq[n, DK:, :] = (fadeq_ref[n] - r[DK:, :DK]).astype(BF16)
            bout[n] = r[DK:, DK:]
        step[...] = gate_ref[...]

    def advance(p, half):
        aq, binp, bout, step = results(p, half)
        states = [carry[h] for h in range(heads)]
        for u in range(UNROLL):
            tokens = slice(half * half_tok + u * BLOCK, half * half_tok + (u + 1) * BLOCK)
            for h in range(heads):
                n = u * heads + h
                gate = step[n : n + 1, :]
                chain = p * heads + h
                if half == 0 and u == 0:
                    trans = jnp.where(before == after, gate, 0.0) + aq[n, 0:DK, :].astype(F32)
                    states[h] = jnp.concatenate([trans, binp[n]], axis=1)
                    m[chain, tokens, :] = aq[n, DK:, :]
                    local[chain, tokens, :] = bout[n].astype(BF16)
                    continue
                r = dot(aq[n], states[h].astype(BF16))
                wide = jnp.concatenate([gate, gate], axis=1)
                inputs = jnp.concatenate([jnp.zeros((DK, DK), F32), binp[n]], axis=1)
                states[h] = wide * states[h] + r[:DK] + inputs
                m[chain, tokens, :] = r[DK:, :DK].astype(BF16)
                local[chain, tokens, :] = (r[DK:, DK:] + bout[n]).astype(BF16)
        for h in range(heads):
            if half == 0:
                carry[h] = states[h]
            else:
                maps[h, p] = states[h].astype(BF16)

    def swap(p):
        return pltpu.make_async_remote_copy(
            maps.at[1 - core, p],
            pair.at[p],
            pair_send.at[p],
            pair_recv.at[p],
            device_id=partner,
            device_id_type=mesh_id,
        )

    def spread(p, d):
        return pltpu.make_async_remote_copy(
            gathered.at[p, chip],
            gathered.at[p, chip],
            x_send.at[p, d - 1],
            x_recv.at[p, d - 1],
            device_id=along_x(d),
            device_id_type=mesh_id,
        )

    def give_back(p):
        return pltpu.make_async_remote_copy(
            back.at[p],
            got.at[p],
            back_send.at[p],
            back_recv.at[p],
            device_id=partner,
            device_id_type=mesh_id,
        )

    def join_pair(p):
        swap(p).wait_recv()
        own = maps[core, p]
        other = pair[p]
        early = jnp.where(core == 0, own, other)
        late = jnp.where(core == 0, other, own)
        both = dot(late[:, :DK], early)
        joined = jnp.concatenate([both[:, :DK], both[:, DK:] + late[:, DK:].astype(F32)], axis=1)
        gathered[p, chip] = joined.astype(BF16)
        for d in range(1, chips):
            spread(p, d).start()

    def compose(p):
        for d in range(1, chips):
            spread(p, d).wait_recv()
        state = gathered[p, 0][:, DK:].astype(F32)
        enter = jnp.where(chip == 1, state, 0.0)
        for k in range(1, chips):
            tk = gathered[p, k]
            state = dot(tk[:, :DK], state.astype(BF16)) + tk[:, DK:].astype(F32)
            if k < chips - 1:
                enter = jnp.where(chip == k + 1, state, enter)
        first_map = jnp.where(core == 0, maps[core, p], pair[p])
        enter = enter.astype(BF16)
        second = (dot(first_map[:, :DK], enter) + first_map[:, DK:].astype(F32)).astype(BF16)
        final = state.astype(BF16)
        finals[core, p] = final
        enters[core, p] = jnp.where(core == 0, enter, second)
        back[p, 0] = jnp.where(core == 0, second, enter)
        back[p, 1] = final
        give_back(p).start()

    def receive(p):
        give_back(p).wait_recv()
        enters[1 - core, p] = got[p, 0]
        finals[1 - core, p] = got[p, 1]

    norm_gain = norm_ref[...]
    stride = 128

    def finish(p):
        length = len_ref[p]

        def tokens(i, _):
            at = pl.ds(pl.multiple_of(i * stride, stride), stride)
            place = s * tok + i * stride + lax.broadcasted_iota(jnp.int32, (stride, DV), 0)
            valid = place < length
            for h in range(heads):
                n = p * heads + h
                raw = dot(m[n, at, :], enters[h, p]) + local[n, at, :].astype(F32)
                scaled = raw * lax.rsqrt(jnp.mean(raw * raw, axis=-1, keepdims=True) + EPSILON)
                zh = z[p, at, h * DV : (h + 1) * DV].astype(F32)
                gated = scaled * norm_gain * silu(zh)
                att[p, at, h * DV : (h + 1) * DV] = jnp.where(valid, gated, 0.0).astype(BF16)
            return 0

        lax.fori_loop(0, tok // stride, tokens, 0, unroll=2)

    load_qk(0).wait()
    load_v(0).wait()
    prepare(0, 1)
    pl.semaphore_wait(barrier, len(peers))
    rims = [
        pltpu.make_async_remote_copy(
            src.at[:, pl.ds(src.shape[1] - RIM, RIM), :],
            dst,
            rim_send.at[i],
            rim_recv.at[i],
            device_id=following,
            device_id_type=mesh_id,
        )
        for i, (src, dst) in enumerate([(qk_hbm, rim_qk), (v_hbm, rim_v)])
    ]
    for rim in rims:
        rim.start()
    for rim in rims:
        rim.wait()

    def prompt(p, _):
        earlier = jnp.maximum(p - 1, 0)
        later = jnp.minimum(p + 1, prompts - 1)
        solve(p, 1)
        prepare(p, 0)
        advance(earlier, 0)

        @pl.when(p < prompts - 1)
        def _():
            load_qk(p + 1).wait()
            load_v(p + 1).wait()

        @pl.when(p >= 2)
        def _():
            join_pair(p - 2)

        solve(p, 0)
        prepare(later, 1)
        advance(earlier, 1)

        @pl.when(p >= 1)
        def _():
            swap(p - 1).start()

        return 0

    lax.fori_loop(0, prompts, prompt, 0)
    last = prompts - 1
    join_pair(last - 1)
    advance(last, 0)
    advance(last, 1)
    swap(last).start()
    for p in range(last - 1):
        compose(p)
    join_pair(last)
    load_z.wait()
    for p in range(last - 1):
        receive(p)
        finish(p)
    compose(last - 1)
    compose(last)
    receive(last - 1)
    receive(last)
    sends = []
    for d in range(1, rows_count):
        to = in_row(d)
        chosen = place_ref[0, to]
        for h in range(heads):
            leaving[d, h] = finals[h, chosen]
        send = pltpu.make_async_remote_copy(
            leaving.at[d],
            roll_hbm.at[row],
            head_send.at[d],
            head_recv.at[d],
            device_id=(s, to),
            device_id_type=mesh_id,
        )
        send.start()
        sends.append(send)
    chosen = place_ref[0, row]
    for h in range(heads):
        leaving[0, h] = finals[h, chosen]
    keep = pltpu.make_async_copy(leaving.at[0], roll_hbm.at[row], own_sem)
    keep.start()
    finish(last - 1)
    finish(last)
    store = pltpu.make_async_copy(att, att_hbm, store_sem)
    store.start()
    for p in range(prompts):
        swap(p).wait_send()
        for d in range(1, chips):
            spread(p, d).wait_send()
        give_back(p).wait_send()
    for send in sends:
        send.wait()
    keep.wait()
    store.wait()


def delta(lengths, placement, qk, v, z, conv_qk, conv_v, log_decay, write_gain, norm_gain, chips, rows_count):
    prompts, tok, width = v.shape
    heads = width // DV
    chains = prompts * heads
    units = UNROLL * heads
    nblk = tok // BLOCK
    smem = pl.BlockSpec(memory_space=pltpu.SMEM)
    hbm = pl.BlockSpec(memory_space=pl.ANY)
    vmem = pl.BlockSpec(memory_space=pltpu.VMEM)
    dma = pltpu.SemaphoreType.DMA

    def twice(*spec):
        return [pltpu.VMEM(*spec), pltpu.VMEM(*spec)]

    return pl.pallas_call(
        delta_kernel,
        in_specs=[smem, smem, hbm, hbm, hbm, vmem, vmem, vmem, vmem, vmem],
        out_specs=[hbm, hbm],
        out_shape=[
            jax.ShapeDtypeStruct((prompts, tok, width), BF16),
            jax.ShapeDtypeStruct((rows_count, heads, DK, DV), BF16),
        ],
        scratch_shapes=[
            pltpu.VMEM(qk.shape, BF16),
            pltpu.VMEM(v.shape, BF16),
            pltpu.VMEM(z.shape, BF16),
            pltpu.VMEM(z.shape, BF16),
            pltpu.VMEM((prompts, RIM, DK), BF16),
            pltpu.VMEM((prompts, RIM, width), BF16),
            pltpu.VMEM((RIM + 2 * UNROLL * BLOCK, DK), F32),
            pltpu.VMEM((heads, RIM + UNROLL * BLOCK, DV), F32),
            pltpu.VMEM((8 * prompts * nblk, BLOCK), F32),
            pltpu.VMEM((chains, tok, DK), BF16),
            pltpu.VMEM((chains, tok, DV), BF16),
            pltpu.VMEM((heads, DK, DK + DV), F32),
            *twice((units, BLOCK, BLOCK), BF16),
            *twice((units, BASE, BLOCK), F32),
            *twice((units, 2 * BLOCK, BLOCK), BF16),
            *twice((units, BLOCK, DK + DV), BF16),
            *twice((units, BLOCK, DK), F32),
            *twice((units, BLOCK), F32),
            pltpu.VMEM((units, 2 * BLOCK, DK), BF16),
            pltpu.VMEM((2, units, 2 * BLOCK, DK), BF16),
            pltpu.VMEM((units, DK, DV), F32),
            pltpu.VMEM((2, units, DK, DV), F32),
            pltpu.VMEM((units, BLOCK, DV), F32),
            pltpu.VMEM((2, units, BLOCK, DV), F32),
            pltpu.VMEM((units, BLOCK), F32),
            pltpu.VMEM((2, units, BLOCK), F32),
            pltpu.VMEM((heads, prompts, DK, DK + DV), BF16),
            pltpu.VMEM((prompts, DK, DK + DV), BF16),
            pltpu.VMEM((prompts, chips, DK, DK + DV), BF16),
            pltpu.VMEM((prompts, 2, DK, DV), BF16),
            pltpu.VMEM((prompts, 2, DK, DV), BF16),
            pltpu.VMEM((heads, prompts, DK, DV), BF16),
            pltpu.VMEM((heads, prompts, DK, DV), BF16),
            pltpu.VMEM((rows_count, heads, DK, DV), BF16),
            dma((prompts,)),
            dma((prompts,)),
            dma,
            dma,
            dma((2,)),
            dma((2,)),
            dma((prompts,)),
            dma((prompts,)),
            dma((prompts, chips - 1)),
            dma((prompts, chips - 1)),
            dma((prompts,)),
            dma((prompts,)),
            dma((rows_count,)),
            dma((rows_count,)),
            dma,
        ],
        compiler_params=pltpu.CompilerParams(
            vmem_limit_bytes=VMEM_LIMIT, collective_id=0, has_side_effects=True
        ),
        name="delta",
    )(lengths, placement, qk, v, z, conv_qk, conv_v, log_decay, write_gain, norm_gain)


def shards(
    qk_in,
    v_in,
    gate_z,
    conv_qk,
    conv_v,
    log_decay,
    write_gain,
    norm_gain,
    prompt_lengths,
    placement,
):
    prompts, tok = v_in.shape[:2]
    heads = log_decay.shape[1]
    head_count = lax.axis_size("head")
    seq_count = lax.axis_size("seq")
    attended, arrived = delta(
        prompt_lengths,
        placement,
        qk_in.reshape(prompts, 2 * tok, DK),
        v_in,
        gate_z,
        conv_qk,
        conv_v,
        log_decay,
        write_gain,
        norm_gain.reshape(1, DV),
        seq_count // 2,
        head_count,
    )
    rollout = arrived.astype(F32).reshape(1, 1, head_count * heads, DK, DV)
    return attended, rollout


def solution(mesh):
    return jax.shard_map(
        shards,
        mesh=mesh,
        in_specs=(
            P(None, "seq", None, "head"),
            P(None, "seq", "head"),
            P(None, "seq", "head"),
            P(None, None, "head"),
            P(None, "head"),
            P(None, "head", "seq"),
            P(None, "head", "seq"),
            P(),
            P(),
            P("seq", None),
        ),
        out_specs=(P(None, "seq", "head"), P("seq", "head", None, None, None)),
        check_vma=False,
    )
```

time: 127 us -> 65.8 us (0.52)
  waiting for transfers between devices: 36.4 us -> 0 us
  blocking collectives: 22.4 us -> 0 us
  Pallas kernels: 42.9 us -> 60.7 us
  between operations: 14.1 us -> 0.65 us
  starting transfers between devices: 4.53 us -> 0 us
  local copies, waits for them, and re-layouts: 3.72 us -> 1.32 us
    all_gather x1 -> x0, waiting for transfers between devices: 35.5 us -> none  [shards(): maps = lax.all_gather(st, 'seq')]
    all_to_all x1 -> x0, blocking collectives: 22.4 us -> none  [shards(): arrived = lax.all_to_all(leaving, 'head', 0, 0, tiled=True)]
    pallas_call x2 -> x1, Pallas kernels: 42.9 us -> 60.7 us  [delta(): pl.pallas_call(delta_kernel, in_specs=[smem, smem, hbm, hbm, hbm, vmem, v...]
    ppermute x1 -> x0, starting transfers between devices: 4.5 us -> none  [shards(): rim = lax.ppermute(tails, 'seq', [(i, i + 1) for i in range(seq_count - 1)])]
    gather x1 -> x0, local copies, waits for them, and re-layouts: 1.7 us -> none  [shards(): leaving = jnp.take(by_prompt, placement[0], axis=0)]
    slice x2 -> x0, local copies, waits for them, and re-layouts: 1.42 us -> none  [the longest x1 0.72 us: shards(): v_in[:, tok - RIM:, h * DV:(h + 1) * DV]]
    reshape x1, other arithmetic: 1.56 us -> 2.94 us  [shards(): rollout = arrived.astype(F32).reshape(1, 1, head_count * heads, DK, DV)]
  transfers between devices with their start and end apart: 2 -> 0, of which waited for: 2 -> 0; matrix products, arithmetic and copies ran while one was open for 0% -> 0% of each run, Pallas kernels for 0% -> 0%
where the time goes in v2:
time: 65.8 us; the launch traced here: 65.6 us
  Pallas kernels  60.7 us (92%)
  other arithmetic  2.94 us (4%)
  local copies, waits for them, and re-layouts  1.32 us (2%)
    pallas_call x1, Pallas kernels, delta(): pl.pallas_call(delta_kernel, in_specs=[smem, smem, hbm, hbm, hbm, vmem, v...  60.7 us
    reshape x1, other arithmetic, shards(): rollout = arrived.astype(F32).reshape(1, 1, head_count * heads, DK, DV)  2.94 us
    unnamed x3, local copies, waits for them, and re-layouts  1.32 us

profile of v2, /device:TPU:1, one launch (start us, length us, event | category | flops | bytes accessed | tf_op | source)
XLA Modules:
  0.0 65.6 jit_solution(7656879905319143112)
XLA Ops:
  0.6 60.7 %delta.1 = (bf16[4,1024,256]{2,1,0:T(8,128)(2,1)}, bf16[16,2,128,128]{3,2,1,0:T(8,128)(2,1)}) custom-call(s32[4]{0:T(128)} %len_ref.1, s32[1,16]{1,0:T(1,128)} %place_ref.1, bf16[4,2048,128]{2,1,0:T(8,128)(2,1)} %bitcast.4, bf16[4,1024,256]{2,1,0:T(8,128)(2,1)} %v_hbm.1, bf16[4,1024,256]{2,1,0:T(8,128)(2,1)} %z_hbm.1, bf16[4,2,128]{2,1,0:T(2,128)(2,1)} %cqk_ref.1, ...), custom_call_target="tpu_custom_call" | custom-call | tf_op jit(solution)/shard_map/delta/pallas_call | solution.py:555
  61.4 0.0 copy-start
  61.4 2.9 %convert.1 = f32[1,1,32,128,128]{4,3,2,1,0:T(8,128)} convert(bf16[1,1,32,128,128]{4,3,2,1,0:T(8,128)(2,1)} %bitcast.5) | non-fusion elementwise | flops 524288 | bytes 3145728 | tf_op jit(solution)/shard_map/reshape | solution.py:651
  64.3 0.0 copy-done
  64.3 1.3 %copy.13 = bf16[4,1024,256]{2,1,0:T(8,128)(2,1)} copy(bf16[4,1024,256]{2,1,0:T(8,128)(2,1)S(1)} %copy-done) | data formatting | bytes 4194304
Async XLA Ops:
  61.4 3.0 %copy-start = (bf16[4,1024,256]{2,1,0:T(8,128)(2,1)S(1)}, bf16[4,1024,256]{2,1,0:T(8,128)(2,1)}, u32[]{:S(2)}) copy-start(bf16[4,1024,256]{2,1,0:T(8,128)(2,1)} %get-tuple-element.8) | copy-start | bytes 6291460

commit v3 on v2

--- a/solution.py
+++ b/solution.py
@@ -15,35 +15,51 @@
 UNROLL = 4
 RIM = 16
 EPSILON = 1e-06
+LOG2E = 1.4426950408889634
 F32 = jnp.float32
 BF16 = jnp.bfloat16
-VMEM_LIMIT = 56 * 1024 * 1024
+VMEM_LIMIT = 28 * 1024 * 1024
 
 
 def dot(a, b):
     return jnp.dot(a, b, preferred_element_type=F32)
 
 
+def silu_of_twice(half):
+    return half + half * jnp.tanh(half)
+
+
 def silu(x):
-    half = 0.5 * x
-    return half + half * jnp.tanh(half)
-
-
-def base_inverses(stricts):
+    return silu_of_twice(0.5 * x)
+
+
+def interleave(*parts):
+    parts = [[0, count, steps] for steps, count in parts]
+    while parts:
+        part = min(parts, key=lambda p: p[0] / p[1])
+        part[0] += 1
+        try:
+            next(part[2])
+        except StopIteration:
+            parts.remove(part)
+
+
+def base_inverses(stricts, masks):
     half = BASE // 2
     lane = lax.broadcasted_iota(jnp.int32, (half, BLOCK), 1)
     row = lax.broadcasted_iota(jnp.int32, (half, BLOCK), 0)
     home = lane // BASE
     tops, bots, lows_top, lows_bot = [], [], [], []
     for s in stricts:
-        top, bot = s[0:half], s[half:BASE]
+        compact = s[0:BASE] * masks[0]
         for b in range(1, BLOCK // BASE):
-            top = jnp.where(home == b, s[b * BASE : b * BASE + half], top)
-            bot = jnp.where(home == b, s[b * BASE + half : (b + 1) * BASE], bot)
-        lows_top.append(top)
-        lows_bot.append(bot)
+            compact = compact + s[b * BASE : (b + 1) * BASE] * masks[b]
+        compact = compact.astype(F32)
+        lows_top.append(compact[:half])
+        lows_bot.append(compact[half:])
         tops.append(jnp.where(lane % BASE == row, 1.0, 0.0).astype(F32))
         bots.append(jnp.where(lane % BASE == row + half, 1.0, 0.0).astype(F32))
+    yield
     for j in range(BASE - 1):
         index = home * BASE + j
         for n in range(len(stricts)):
@@ -51,45 +67,78 @@
             if j < half - 1:
                 tops[n] = tops[n] - jnp.take_along_axis(lows_top[n], index, axis=1) * source
             bots[n] = bots[n] - jnp.take_along_axis(lows_bot[n], index, axis=1) * source
+        yield
     return [jnp.concatenate([t, b], axis=0) for t, b in zip(tops, bots)]
 
 
-def merge_levels(slabs, lows):
+def lane_masks(size):
+    home = lax.broadcasted_iota(jnp.int32, (size, BLOCK), 1) // size
+    return [jnp.where(home == b, 1.0, 0.0).astype(BF16) for b in range(BLOCK // size)]
+
+
+def stacked_products(lefts, rights):
+    out = []
+    for n in range(0, len(lefts), 2):
+        size = lefts[n].shape[0]
+        both = dot(
+            jnp.concatenate(lefts[n : n + 2], axis=0), jnp.concatenate(rights[n : n + 2], axis=1)
+        )
+        out += [both[:size, :BLOCK].astype(BF16), both[size:, BLOCK:].astype(BF16)]
+        yield
+    return out
+
+
+def merge_blocks(inverses, lows):
     size = BASE
     while size < BLOCK // 2:
-        per = size // BASE
-        lane_slab = lax.broadcasted_iota(jnp.int32, (size, BLOCK), 1) // size
-        odd = [o for o in range(1, BLOCK // size, 2)]
-        lefts = [
-            jnp.concatenate([slab for o in odd for slab in sl[o * per : (o + 1) * per]], axis=0)
-            for sl in slabs
+        masks = lane_masks(size)
+        count = BLOCK // size
+        evens = sum(masks[2::2], masks[0])
+        odds = sum(masks[3::2], masks[1])
+        zeros = jnp.zeros((size, BLOCK), BF16)
+        below = [
+            jnp.concatenate(
+                [
+                    low[o * size : (o + 1) * size] * masks[o - 1] if o % 2 else zeros
+                    for o in range(count)
+                ],
+                axis=0,
+            )
+            for low in lows
         ]
-        wholes = [jnp.concatenate(sl, axis=0) for sl in slabs]
-        keep = jnp.concatenate([(lane_slab == o - 1).astype(F32) for o in odd], axis=0) > 0.5
-        ys = [jnp.where(keep, dot(a, low), 0.0).astype(BF16) for a, low in zip(lefts, lows)]
-        zs = [dot(y, w) for y, w in zip(ys, wholes)]
-        for n, z in enumerate(zs):
-            new = (lefts[n].astype(F32) - z).astype(BF16)
-            for m, o in enumerate(odd):
-                for i in range(per):
-                    at = m * size + i * BASE
-                    slabs[n][o * per + i] = new[at : at + BASE]
+        above = [
+            jnp.concatenate([zeros if e % 2 else x * masks[e] for e in range(count)], axis=0)
+            for x in inverses
+        ]
+        ys = yield from stacked_products(inverses, below)
+        zs = yield from stacked_products(ys, above)
+        inverses = [
+            jnp.concatenate([x * evens, x * odds - z], axis=0) for x, z in zip(inverses, zs)
+        ]
         size *= 2
+    return inverses
 
 
 def delta_kernel(
-    len_ref,
-    place_ref,
+    len_hbm,
+    place_hbm,
     qk_hbm,
     v_hbm,
     z_hbm,
+    cqk_hbm,
+    cv_hbm,
+    ld_hbm,
+    wg_hbm,
+    norm_hbm,
+    att_hbm,
+    roll_hbm,
+    len_ref,
+    place_ref,
     cqk_ref,
     cv_ref,
     ld_ref,
     wg_ref,
     norm_ref,
-    att_hbm,
-    roll_hbm,
     qk,
     v,
     z,
@@ -108,12 +157,14 @@
     base_b,
     left_a,
     left_b,
-    both_a,
-    both_b,
-    fadeq_a,
-    fadeq_b,
-    gate_a,
-    gate_b,
+    query_a,
+    query_b,
+    key_a,
+    key_b,
+    value_a,
+    value_b,
+    scale_a,
+    scale_b,
     aq_0,
     aq_1,
     binp_0,
@@ -145,6 +196,7 @@
     head_send,
     head_recv,
     own_sem,
+    small_sem,
 ):
     prompts, tok = v.shape[:2]
     heads = ld_ref.shape[1]
@@ -162,8 +214,8 @@
     following = (lax.rem(s + 1, seq_count), row)
     preceding = (lax.rem(s + seq_count - 1, seq_count), row)
     sets = {
-        1: (strict_b, base_b, left_b, both_b, fadeq_b, gate_b),
-        0: (strict_a, base_a, left_a, both_a, fadeq_a, gate_a),
+        1: (strict_b, base_b, left_b, query_b, key_b, value_b, scale_b),
+        0: (strict_a, base_a, left_a, query_a, key_a, value_a, scale_a),
     }
 
     def results(p, half):
@@ -184,10 +236,24 @@
         return pltpu.make_async_copy(v_hbm.at[p], v.at[p], v_sem.at[p])
 
     load_z = pltpu.make_async_copy(z_hbm, z, z_sem)
-    for p in range(prompts):
-        load_qk(p).start()
-        load_v(p).start()
-    load_z.start()
+    small = [
+        pltpu.make_async_copy(src, dst, small_sem.at[i])
+        for i, (src, dst) in enumerate(
+            [
+                (len_hbm, len_ref),
+                (ld_hbm, ld_ref),
+                (wg_hbm, wg_ref),
+                (cqk_hbm, cqk_ref),
+                (cv_hbm, cv_ref),
+                (place_hbm, place_ref),
+                (norm_hbm, norm_ref),
+            ]
+        )
+    ]
+    for copy in small:
+        copy.start()
+    load_qk(0).start()
+    load_v(0).start()
     barrier = pltpu.get_barrier_semaphore()
     peers = [following, preceding]
     peers += [along_x(d) for d in range(1, chips)]
@@ -201,6 +267,8 @@
     strictly = before > after
     upto = jnp.where(before <= after, 1.0, 0.0).astype(F32)
     rows[...] = jnp.zeros_like(rows)
+    for copy in small:
+        copy.wait()
     position = lax.broadcasted_iota(jnp.int32, (heads, tok), 1) + s * tok
     for p in range(prompts):
         valid = position < len_ref[p]
@@ -213,12 +281,14 @@
     raw_rows = rows[...]
     sums = jnp.dot(raw_rows, upto, precision=lax.Precision.HIGHEST, preferred_element_type=F32)
     kind = lax.broadcasted_iota(jnp.int32, raw_rows.shape, 0) % 8
-    rows[...] = jnp.where(kind < heads, sums, raw_rows)
-    taps_qk = cqk_ref[...].astype(F32)
-    taps_v = cv_ref[...].astype(F32)
+    rows[...] = jnp.where(kind < heads, sums * LOG2E, raw_rows)
+    half_taps_qk = 0.5 * cqk_ref[...].astype(F32)
+    half_taps_v = 0.5 * cv_ref[...].astype(F32)
+    masks = lane_masks(BASE)
+    ones = jnp.ones((DK, DK), BF16)
 
     def prepare(p, half):
-        strict_ref, base_ref, left_ref, both_ref, fadeq_ref, gate_ref = sets[half]
+        strict_ref, base_ref, left_ref, query_ref, key_ref, value_ref, scale_ref = sets[half]
         blocks = range(UNROLL)
         start = half * half_tok
         if half == 0:
@@ -234,95 +304,99 @@
             else:
                 xv[h, 0:RIM, :] = v[p, start - RIM : start, lanes].astype(F32)
             xv[h, RIM:, :] = v[p, start : start + half_tok, lanes].astype(F32)
+        yield
 
         def mixed(u, which):
             total = None
             for i in range(CONV):
                 at = RIM + 2 * (u * BLOCK - (CONV - 1) + i) + which
-                term = xqk[pl.ds(at, BLOCK, stride=2), :] * taps_qk[i, which : which + 1, :]
+                term = xqk[pl.ds(at, BLOCK, stride=2), :] * half_taps_qk[i, which : which + 1, :]
                 total = term if total is None else total + term
-            return silu(total)
-
-        def unit(x):
-            return x * lax.rsqrt(jnp.sum(x * x, axis=-1, keepdims=True) + EPSILON)
-
-        queries, keys, keys_t, values, tiles, columns = [], [], [], [], [], []
+            return silu_of_twice(total)
+
+        squares, mixes = [], []
         for u in blocks:
-            q = unit(mixed(u, 0))
-            k = unit(mixed(u, 1))
-            queries.append(q.astype(BF16))
-            keys.append(k.astype(BF16))
+            mixes.append((mixed(u, 0), mixed(u, 1)))
+            both = jnp.concatenate(mixes[u], axis=0)
+            squares.append((both * both).astype(BF16))
+            yield
+        totals = [dot(sq, ones) for sq in squares]
+        yield
+        keys_t = []
+        for u in blocks:
+            q, k = mixes[u]
+            query_ref[u] = (q * lax.rsqrt(totals[u][:BLOCK] + EPSILON)).astype(BF16)
+            k = k * lax.rsqrt(totals[u][BLOCK:] + EPSILON)
+            key_ref[u] = k.astype(BF16)
             keys_t.append(k.T.astype(BF16))
-            vs = []
+            yield
+        grams = []
+        for u in blocks:
+            grams.append(dot(jnp.concatenate([query_ref[u], key_ref[u]], axis=0), keys_t[u]))
+            yield
+        stricts = []
+        for u in blocks:
+            at = pl.multiple_of(8 * (p * nblk + half * UNROLL + u), 8)
+            tile = rows[pl.ds(at, 8), :]
+            column = tile.T
+            query_key = jnp.where(lower, grams[u][:BLOCK], 0.0).astype(BF16)
+            key_key = jnp.where(strictly, grams[u][BLOCK:], 0.0).astype(BF16)
             for h in range(heads):
+                n = u * heads + h
+                middle = 0.5 * tile[h : h + 1, BLOCK - 1 : BLOCK]
+                gain = tile[heads + h : heads + h + 1].astype(BF16)
+                strict = key_key * gain
+                stricts.append(strict)
+                strict_ref[n] = strict
+                left_ref[n, 0:DK, :] = keys_t[u] * gain
+                left_ref[n, DK:, :] = query_key * gain
+                growth = jnp.exp2(middle - column[:, h : h + 1])
                 total = None
                 for i in range(CONV):
                     at = RIM + u * BLOCK - (CONV - 1) + i
-                    term = xv[h, at : at + BLOCK, :] * taps_v[i : i + 1, h * DV : (h + 1) * DV]
+                    term = xv[h, at : at + BLOCK, :] * half_taps_v[i : i + 1, h * DV : (h + 1) * DV]
                     total = term if total is None else total + term
-                vs.append(silu(total).astype(BF16))
-            values.append(vs)
-            at = pl.multiple_of(8 * (p * nblk + half * UNROLL + u), 8)
-            tile = rows[pl.ds(at, 8), :]
-            tiles.append(tile)
-            columns.append(tile.T)
-        grams = [dot(jnp.concatenate([queries[u], keys[u]], axis=0), keys_t[u]) for u in blocks]
-        stricts = []
-        for u in blocks:
-            query_key = grams[u][:BLOCK]
-            key_key = jnp.where(strictly, grams[u][BLOCK:], 0.0)
-            for h in range(heads):
-                n = u * heads + h
-                cum_row = tiles[u][h : h + 1]
-                last = cum_row[:, BLOCK - 1 : BLOCK]
-                cum = jnp.broadcast_to(columns[u][:, h : h + 1], (BLOCK, BLOCK))
-                gb = jnp.broadcast_to(columns[u][:, heads + h : heads + h + 1], (BLOCK, BLOCK))
-                ratio = jnp.exp(jnp.where(lower, cum - cum_row, -1e30))
-                fade = jnp.exp(cum)
-                strict = ratio * key_key * gb
-                stricts.append(strict)
-                strict_ref[n] = strict.astype(BF16)
-                left_ref[n, 0:DK, :] = (
-                    keys_t[u].astype(F32) * jnp.exp(last - cum_row)
-                ).astype(BF16)
-                left_ref[n, DK:, :] = (ratio * query_key).astype(BF16)
-                both_ref[n, :, 0:DK] = (keys[u].astype(F32) * (gb * fade)).astype(BF16)
-                both_ref[n, :, DK:] = (values[u][h].astype(F32) * gb).astype(BF16)
-                fadeq_ref[n] = queries[u].astype(F32) * fade
-                gate_ref[n : n + 1, :] = jnp.broadcast_to(jnp.exp(last), (1, BLOCK))
-        for n, x in enumerate(base_inverses(stricts)):
-            base_ref[n] = x
+                value_ref[n] = (silu_of_twice(total) * growth).astype(BF16)
+                scale_ref[n : n + 1, :] = jnp.broadcast_to(jnp.exp2(middle), (1, BLOCK))
+                yield
+        found = yield from base_inverses(stricts, masks)
+        for n, x in enumerate(found):
+            base_ref[n] = x.astype(BF16)
 
     def solve(p, half):
-        strict_ref, base_ref, left_ref, both_ref, fadeq_ref, gate_ref = sets[half]
+        strict_ref, base_ref, left_ref, query_ref, key_ref, value_ref, scale_ref = sets[half]
         aq, binp, bout, step = results(p, half)
         units = range(UNROLL * heads)
         mid = BLOCK // 2
-        home = lax.broadcasted_iota(jnp.int32, (BASE, BLOCK), 1) // BASE
         lows = [strict_ref[n] for n in units]
-        slabs = []
+        inverses = yield from merge_blocks([base_ref[n] for n in units], lows)
+        tops = [x[:, :mid] for x in inverses]
+        bots = [x[:, mid:] for x in inverses]
+        def written(n, block):
+            return jnp.concatenate([key_ref[n // heads, block, :], value_ref[n, block, :]], axis=1)
+
+        w1, rest, w2 = [], [], []
         for n in units:
-            x = base_ref[n]
-            slabs.append(
-                [jnp.where(home == b, x, 0.0).astype(BF16) for b in range(BLOCK // BASE)]
-            )
-        merge_levels(slabs, lows)
-        per = mid // BASE
-        tops = [jnp.concatenate(sl[:per], axis=0)[:, :mid] for sl in slabs]
-        bots = [jnp.concatenate(sl[per:], axis=0)[:, mid:] for sl in slabs]
-        w1 = [dot(tops[n], both_ref[n, 0:mid, :]).astype(BF16) for n in units]
-        rest = [
-            (both_ref[n, mid:, :].astype(F32) - dot(lows[n][mid:, :mid], w1[n])).astype(BF16)
-            for n in units
-        ]
-        w2 = [dot(bots[n], rest[n]).astype(BF16) for n in units]
+            w1.append(dot(tops[n], written(n, slice(0, mid))).astype(BF16))
+            if n % 2:
+                yield
+        for n in units:
+            below = written(n, slice(mid, BLOCK)).astype(F32)
+            rest.append((below - dot(lows[n][mid:, :mid], w1[n])).astype(BF16))
+            if n % 2:
+                yield
+        for n in units:
+            w2.append(dot(bots[n], rest[n]).astype(BF16))
+            if n % 2:
+                yield
         for n in units:
             r = dot(left_ref[n], jnp.concatenate([w1[n], w2[n]], axis=0))
             aq[n, 0:DK, :] = (-r[:DK, :DK]).astype(BF16)
-            binp[n] = r[:DK, DK:]
-            aq[n, DK:, :] = (fadeq_ref[n] - r[DK:, :DK]).astype(BF16)
+            binp[n] = r[:DK, DK:] * scale_ref[n : n + 1, :]
+            aq[n, DK:, :] = (query_ref[n // heads].astype(F32) - r[DK:, :DK]).astype(BF16)
             bout[n] = r[DK:, DK:]
-        step[...] = gate_ref[...]
+            yield
+        step[...] = scale_ref[...]
 
     def advance(p, half):
         aq, binp, bout, step = results(p, half)
@@ -331,25 +405,31 @@
             tokens = slice(half * half_tok + u * BLOCK, half * half_tok + (u + 1) * BLOCK)
             for h in range(heads):
                 n = u * heads + h
-                gate = step[n : n + 1, :]
+                scale = step[n : n + 1, :]
+                gate = scale * scale
                 chain = p * heads + h
                 if half == 0 and u == 0:
-                    trans = jnp.where(before == after, gate, 0.0) + aq[n, 0:DK, :].astype(F32)
-                    states[h] = jnp.concatenate([trans, binp[n]], axis=1)
-                    m[chain, tokens, :] = aq[n, DK:, :]
+                    trans = jnp.where(before == after, 1.0, 0.0) + aq[n, 0:DK, :].astype(F32)
+                    states[h] = jnp.concatenate([trans * gate, binp[n]], axis=1)
+                    m[chain, tokens, :] = (aq[n, DK:, :].astype(F32) * scale).astype(BF16)
                     local[chain, tokens, :] = bout[n].astype(BF16)
                     continue
                 r = dot(aq[n], states[h].astype(BF16))
                 wide = jnp.concatenate([gate, gate], axis=1)
                 inputs = jnp.concatenate([jnp.zeros((DK, DK), F32), binp[n]], axis=1)
-                states[h] = wide * states[h] + r[:DK] + inputs
-                m[chain, tokens, :] = r[DK:, :DK].astype(BF16)
-                local[chain, tokens, :] = (r[DK:, DK:] + bout[n]).astype(BF16)
+                states[h] = wide * (states[h] + r[:DK]) + inputs
+                m[chain, tokens, :] = (r[DK:, :DK] * scale).astype(BF16)
+                local[chain, tokens, :] = (r[DK:, DK:] * scale + bout[n]).astype(BF16)
+            yield
         for h in range(heads):
             if half == 0:
                 carry[h] = states[h]
             else:
                 maps[h, p] = states[h].astype(BF16)
+
+    def chain_steps(p):
+        yield from advance(p, 0)
+        yield from advance(p, 1)
 
     def swap(p):
         return pltpu.make_async_remote_copy(
@@ -419,29 +499,39 @@
         finals[1 - core, p] = got[p, 1]
 
     norm_gain = norm_ref[...]
-    stride = 128
+    average = jnp.full((DV, DV), 1.0 / DV, BF16)
 
     def finish(p):
-        length = len_ref[p]
-
-        def tokens(i, _):
-            at = pl.ds(pl.multiple_of(i * stride, stride), stride)
-            place = s * tok + i * stride + lax.broadcasted_iota(jnp.int32, (stride, DV), 0)
-            valid = place < length
-            for h in range(heads):
-                n = p * heads + h
-                raw = dot(m[n, at, :], enters[h, p]) + local[n, at, :].astype(F32)
-                scaled = raw * lax.rsqrt(jnp.mean(raw * raw, axis=-1, keepdims=True) + EPSILON)
+        def part(i, _):
+            places, fades, raws = [], [], []
+            for u in range(UNROLL):
+                c = i * UNROLL + u
+                at = pl.ds(pl.multiple_of(c * BLOCK, BLOCK), BLOCK)
+                tile = rows[pl.ds(pl.multiple_of(8 * (p * nblk + c), 8), 8), :]
+                column = tile.T
+                for h in range(heads):
+                    n = p * heads + h
+                    middle = 0.5 * tile[h : h + 1, BLOCK - 1 : BLOCK]
+                    places.append((at, h))
+                    fades.append(jnp.exp2(column[:, h : h + 1] - middle))
+                    raws.append(dot(m[n, at, :], enters[h, p]) + local[n, at, :].astype(F32))
+            raws = [raw * fade for raw, fade in zip(raws, fades)]
+            means = [dot((raw * raw).astype(BF16), average) for raw in raws]
+            for (at, h), raw, mean in zip(places, raws, means):
                 zh = z[p, at, h * DV : (h + 1) * DV].astype(F32)
-                gated = scaled * norm_gain * silu(zh)
-                att[p, at, h * DV : (h + 1) * DV] = jnp.where(valid, gated, 0.0).astype(BF16)
+                gated = raw * lax.rsqrt(mean + EPSILON) * norm_gain * silu(zh)
+                att[p, at, h * DV : (h + 1) * DV] = gated.astype(BF16)
             return 0
 
-        lax.fori_loop(0, tok // stride, tokens, 0, unroll=2)
+        lax.fori_loop(0, nblk // UNROLL, part, 0)
 
     load_qk(0).wait()
     load_v(0).wait()
-    prepare(0, 1)
+    for p in range(1, prompts):
+        load_qk(p).start()
+        load_v(p).start()
+    load_z.start()
+    interleave((prepare(0, 1), 1))
     pl.semaphore_wait(barrier, len(peers))
     rims = [
         pltpu.make_async_remote_copy(
@@ -456,40 +546,29 @@
     ]
     for rim in rims:
         rim.start()
+    interleave((solve(0, 1), 1))
     for rim in rims:
         rim.wait()
+    interleave((prepare(0, 0), 1))
 
     def prompt(p, _):
-        earlier = jnp.maximum(p - 1, 0)
-        later = jnp.minimum(p + 1, prompts - 1)
-        solve(p, 1)
-        prepare(p, 0)
-        advance(earlier, 0)
-
-        @pl.when(p < prompts - 1)
-        def _():
-            load_qk(p + 1).wait()
-            load_v(p + 1).wait()
-
-        @pl.when(p >= 2)
-        def _():
-            join_pair(p - 2)
-
-        solve(p, 0)
-        prepare(later, 1)
-        advance(earlier, 1)
+        load_qk(p + 1).wait()
+        load_v(p + 1).wait()
+        interleave((solve(p, 0), 37), (prepare(p + 1, 1), 38))
 
         @pl.when(p >= 1)
         def _():
-            swap(p - 1).start()
-
+            join_pair(p - 1)
+
+        interleave((solve(p + 1, 1), 37), (prepare(p + 1, 0), 38), (chain_steps(p), 8))
+        swap(p).start()
         return 0
 
-    lax.fori_loop(0, prompts, prompt, 0)
     last = prompts - 1
+    lax.fori_loop(0, last, prompt, 0)
+    interleave((solve(last, 0), 1))
     join_pair(last - 1)
-    advance(last, 0)
-    advance(last, 1)
+    interleave((chain_steps(last), 1))
     swap(last).start()
     for p in range(last - 1):
         compose(p)
@@ -544,9 +623,7 @@
     chains = prompts * heads
     units = UNROLL * heads
     nblk = tok // BLOCK
-    smem = pl.BlockSpec(memory_space=pltpu.SMEM)
     hbm = pl.BlockSpec(memory_space=pl.ANY)
-    vmem = pl.BlockSpec(memory_space=pltpu.VMEM)
     dma = pltpu.SemaphoreType.DMA
 
     def twice(*spec):
@@ -554,13 +631,20 @@
 
     return pl.pallas_call(
         delta_kernel,
-        in_specs=[smem, smem, hbm, hbm, hbm, vmem, vmem, vmem, vmem, vmem],
+        in_specs=[hbm] * 10,
         out_specs=[hbm, hbm],
         out_shape=[
             jax.ShapeDtypeStruct((prompts, tok, width), BF16),
             jax.ShapeDtypeStruct((rows_count, heads, DK, DV), BF16),
         ],
         scratch_shapes=[
+            pltpu.SMEM(lengths.shape, jnp.int32),
+            pltpu.SMEM(placement.shape, jnp.int32),
+            pltpu.VMEM(conv_qk.shape, BF16),
+            pltpu.VMEM(conv_v.shape, BF16),
+            pltpu.VMEM(log_decay.shape, F32),
+            pltpu.VMEM(write_gain.shape, F32),
+            pltpu.VMEM(norm_gain.shape, F32),
             pltpu.VMEM(qk.shape, BF16),
             pltpu.VMEM(v.shape, BF16),
             pltpu.VMEM(z.shape, BF16),
@@ -574,10 +658,11 @@
             pltpu.VMEM((chains, tok, DV), BF16),
             pltpu.VMEM((heads, DK, DK + DV), F32),
             *twice((units, BLOCK, BLOCK), BF16),
-            *twice((units, BASE, BLOCK), F32),
+            *twice((units, BASE, BLOCK), BF16),
             *twice((units, 2 * BLOCK, BLOCK), BF16),
-            *twice((units, BLOCK, DK + DV), BF16),
-            *twice((units, BLOCK, DK), F32),
+            *twice((UNROLL, BLOCK, DK), BF16),
+            *twice((UNROLL, BLOCK, DK), BF16),
+            *twice((units, BLOCK, DV), BF16),
             *twice((units, BLOCK), F32),
             pltpu.VMEM((units, 2 * BLOCK, DK), BF16),
             pltpu.VMEM((2, units, 2 * BLOCK, DK), BF16),
@@ -610,6 +695,7 @@
             dma((rows_count,)),
             dma((rows_count,)),
             dma,
+            dma((7,)),
         ],
         compiler_params=pltpu.CompilerParams(
             vmem_limit_bytes=VMEM_LIMIT, collective_id=0, has_side_effects=True
@@ -634,7 +720,7 @@
     heads = log_decay.shape[1]
     head_count = lax.axis_size("head")
     seq_count = lax.axis_size("seq")
-    attended, arrived = delta(
+    arguments = (
         prompt_lengths,
         placement,
         qk_in.reshape(prompts, 2 * tok, DK),
@@ -645,9 +731,12 @@
         log_decay,
         write_gain,
         norm_gain.reshape(1, DV),
-        seq_count // 2,
-        head_count,
     )
+    arguments = [pltpu.with_memory_space_constraint(a, pltpu.HBM) for a in arguments]
+    attended, arrived = delta(*arguments, seq_count // 2, head_count)
+    position = lax.broadcasted_iota(jnp.int32, attended.shape, 1) + lax.axis_index("seq") * tok
+    limit = lax.broadcast_in_dim(prompt_lengths, attended.shape, (0,))
+    attended = jnp.where(position < limit, attended, 0).astype(BF16)
     rollout = arrived.astype(F32).reshape(1, 1, head_count * heads, DK, DV)
     return attended, rollout
 

time: 65.8 us -> 56.6 us (0.86)
  the two profiles are of different devices: /device:TPU:1 before, /device:TPU:101 now
where the time goes in v3:
time: 56.6 us; the launch traced here: 56.4 us
  Pallas kernels  52.2 us (92%)
  other arithmetic  3.55 us (6%)
  between operations  0.67 us (1%)
    pallas_call x1, Pallas kernels, delta(): pl.pallas_call(delta_kernel, in_specs=[hbm] * 10, out_specs=[hbm, hbm], o...  52.2 us
    select_n x1, other arithmetic, shards(): attended = jnp.where(position < limit, attended, 0).astype(BF16)  1.98 us
    reshape x1, other arithmetic, shards(): rollout = arrived.astype(F32).reshape(1, 1, head_count * heads, DK, DV)  1.56 us

profile of v3, /device:TPU:101, one launch (start us, length us, event | category | flops | bytes accessed | tf_op | source)
XLA Modules:
  0.0 56.4 jit_solution(7364076387890907700)
XLA Ops:
  0.6 0.0 copy-start
  0.7 52.2 %delta.1 = (bf16[4,1024,256]{2,1,0:T(8,128)(2,1)S(1)}, bf16[16,2,128,128]{3,2,1,0:T(8,128)(2,1)S(1)}) custom-call(s32[4]{0:T(128)} %len_hbm.1, s32[1,16]{1,0:T(1,128)} %place_hbm.1, bf16[4,2048,128]{2,1,0:T(8,128)(2,1)} %bitcast.5, bf16[4,1024,256]{2,1,0:T(8,128)(2,1)} %v_hbm.1, bf16[4,1024,256]{2,1,0:T(8,128)(2,1)} %z_hbm.1, bf16[4,2,128]{2,1,0:T(2,128)(2,1)} %cqk_hbm.1, ...), custom_call_target="tpu_custom_call" | custom-call | tf_op jit(solution)/shard_map/delta/pallas_call | solution.py:632
  52.9 0.0 copy-done
  52.9 2.0 %compare_select_fusion = bf16[4,1024,256]{2,1,0:T(8,128)(2,1)} fusion(bf16[4,1024,256]{2,1,0:T(8,128)(2,1)S(1)} %get-tuple-element.4, s32[4]{0:T(128)S(1)} %copy-done, s32[1024]{0:T(1024)S(1)} %iota_add_fusion), kind=kLoop, calls=%fused_computation | loop fusion | flops 2097152 | bytes 4198416 | tf_op jit(solution)/shard_map/jit(_where)/select_n | solution.py:739
  54.9 1.6 %convert.1 = f32[1,1,32,128,128]{4,3,2,1,0:T(8,128)} convert(bf16[1,1,32,128,128]{4,3,2,1,0:T(8,128)(2,1)S(1)} %bitcast.4) | non-fusion elementwise | flops 524288 | bytes 3145728 | tf_op jit(solution)/shard_map/reshape | solution.py:740
  (1 shorter events, 0.0 us)
Async XLA Ops:
  0.6 52.2 %copy-start = (s32[4]{0:T(128)S(1)}, s32[4]{0:T(128)}, u32[]{:S(2)}) copy-start(s32[4]{0:T(128)} %len_hbm.1) | copy-start | bytes 52

commit v4 on v3

--- a/solution.py
+++ b/solution.py
@@ -1,4 +1,4 @@
-import functools
+import math
 
 import jax
 import jax.numpy as jnp
@@ -18,7 +18,7 @@
 LOG2E = 1.4426950408889634
 F32 = jnp.float32
 BF16 = jnp.bfloat16
-VMEM_LIMIT = 28 * 1024 * 1024
+VMEM_LIMIT = 40 * 1024 * 1024
 
 
 def dot(a, b):
@@ -179,8 +179,12 @@
     back,
     got,
     enters,
-    finals,
-    leaving,
+    by_y,
+    by_z,
+    picked,
+    handed,
+    wish,
+    wished,
     qk_sem,
     v_sem,
     z_sem,
@@ -193,9 +197,15 @@
     x_recv,
     back_send,
     back_recv,
-    head_send,
-    head_recv,
-    own_sem,
+    near_send,
+    near_recv,
+    far_send,
+    far_recv,
+    hand_send,
+    hand_recv,
+    keep_sem,
+    wish_send,
+    wish_recv,
     small_sem,
 ):
     prompts, tok = v.shape[:2]
@@ -203,7 +213,7 @@
     nblk = tok // BLOCK
     half_tok = UNROLL * BLOCK
     chips = gathered.shape[1]
-    rows_count = leaving.shape[0]
+    side = by_y.shape[1]
     seq_count = 2 * chips
     s = lax.axis_index("seq")
     row = lax.axis_index("head")
@@ -226,8 +236,14 @@
     def along_x(d):
         return (lax.rem(chip + d, chips) * 2 + core, row)
 
-    def in_row(d):
-        return lax.rem(row + d, rows_count)
+    at_y = lax.div(row, side)
+    at_z = lax.rem(row, side)
+
+    def along_y(d):
+        return (s, lax.rem(at_y + d, side) * side + at_z)
+
+    def along_z(d):
+        return (s, at_y * side + lax.rem(at_z + d, side))
 
     def load_qk(p):
         return pltpu.make_async_copy(qk_hbm.at[p], qk.at[p], qk_sem.at[p])
@@ -257,7 +273,8 @@
     barrier = pltpu.get_barrier_semaphore()
     peers = [following, preceding]
     peers += [along_x(d) for d in range(1, chips)]
-    peers += [(s, in_row(d)) for d in range(1, rows_count)]
+    peers += [along_y(d) for d in range(1, side)]
+    peers += [along_z(d) for d in range(1, side)]
     for peer in peers:
         pl.semaphore_signal(barrier, inc=1, device_id=peer, device_id_type=mesh_id)
 
@@ -487,16 +504,92 @@
         enter = enter.astype(BF16)
         second = (dot(first_map[:, :DK], enter) + first_map[:, DK:].astype(F32)).astype(BF16)
         final = state.astype(BF16)
-        finals[core, p] = final
+        mid = DK // 2
+        by_y[p, at_y, at_z] = final[:mid]
+        by_z[p, at_z, at_y] = final[mid:]
+        for copy in near(p):
+            copy.start()
         enters[core, p] = jnp.where(core == 0, enter, second)
-        back[p, 0] = jnp.where(core == 0, second, enter)
-        back[p, 1] = final
+        back[p] = jnp.where(core == 0, second, enter)
         give_back(p).start()
+
+    def near(p):
+        copies = []
+        for d in range(1, side):
+            for way, (block, to) in enumerate(
+                [(by_y.at[p, at_y, at_z], along_z(d)), (by_z.at[p, at_z, at_y], along_y(d))]
+            ):
+                copies.append(
+                    pltpu.make_async_remote_copy(
+                        block,
+                        block,
+                        near_send.at[p, way, d - 1],
+                        near_recv.at[p, way, d - 1],
+                        device_id=to,
+                        device_id_type=mesh_id,
+                    )
+                )
+        return copies
+
+    def far(p):
+        copies = []
+        for d in range(1, side):
+            for way, (block, to) in enumerate(
+                [(by_y.at[p, at_y], along_y(d)), (by_z.at[p, at_z], along_z(d))]
+            ):
+                copies.append(
+                    pltpu.make_async_remote_copy(
+                        block,
+                        block,
+                        far_send.at[p, way, d - 1],
+                        far_recv.at[p, way, d - 1],
+                        device_id=to,
+                        device_id_type=mesh_id,
+                    )
+                )
+        return copies
+
+    def relay(p):
+        for copy in near(p):
+            copy.wait_recv()
+        for copy in far(p):
+            copy.start()
+
+    def spot(way, i):
+        if way == 0:
+            return roll_hbm.at[i, :, core, 0 : DK // 2]
+        return roll_hbm.at[:, i, core, DK // 2 : DK]
+
+    def line(way, d):
+        return lax.rem((at_y, at_z)[way] + d, side)
+
+    def hand(way, d):
+        i = line(way, d)
+        return pltpu.make_async_remote_copy(
+            handed.at[way, i],
+            spot(way, i),
+            hand_send.at[way, d],
+            hand_recv.at[way, d],
+            device_id=partner,
+            device_id_type=mesh_id,
+        )
+
+    def keep(way, d):
+        i = line(way, d)
+        return pltpu.make_async_copy(picked.at[way, i], spot(way, i), keep_sem.at[way, d])
+
+    def pick(chosen, target, way, d):
+        i = line(way, d)
+        blocks = (by_y, by_z)[way]
+        for at in range(side):
+            block = blocks[0, i, at]
+            for p in range(1, prompts):
+                block = jnp.where(chosen == p, blocks[p, i, at], block)
+            target[way, i, at] = block
 
     def receive(p):
         give_back(p).wait_recv()
-        enters[1 - core, p] = got[p, 0]
-        finals[1 - core, p] = got[p, 1]
+        enters[1 - core, p] = got[p]
 
     norm_gain = norm_ref[...]
     average = jnp.full((DV, DV), 1.0 / DV, BF16)
@@ -551,6 +644,12 @@
         rim.wait()
     interleave((prepare(0, 0), 1))
 
+    tell = pltpu.make_async_remote_copy(
+        wish, wished, wish_send, wish_recv, device_id=partner, device_id_type=mesh_id
+    )
+    wish[...] = jnp.full(wish.shape, place_ref[0, row], jnp.int32)
+    tell.start()
+
     def prompt(p, _):
         load_qk(p + 1).wait()
         load_v(p + 1).wait()
@@ -560,60 +659,73 @@
         def _():
             join_pair(p - 1)
 
+        @pl.when(p >= 2)
+        def _():
+            compose(p - 2)
+
         interleave((solve(p + 1, 1), 37), (prepare(p + 1, 0), 38), (chain_steps(p), 8))
         swap(p).start()
+
+        @pl.when(p >= 2)
+        def _():
+            relay(p - 2)
+
         return 0
 
     last = prompts - 1
     lax.fori_loop(0, last, prompt, 0)
     interleave((solve(last, 0), 1))
     join_pair(last - 1)
+    compose(last - 2)
     interleave((chain_steps(last), 1))
     swap(last).start()
-    for p in range(last - 1):
-        compose(p)
+    load_z.wait()
+    relay(last - 2)
+    receive(0)
+    finish(0)
     join_pair(last)
-    load_z.wait()
-    for p in range(last - 1):
-        receive(p)
-        finish(p)
     compose(last - 1)
+    receive(1)
+    finish(1)
+    relay(last - 1)
     compose(last)
     receive(last - 1)
+    finish(last - 1)
+    relay(last)
+    tell.wait()
+    theirs = wished[0, 0]
+    mine = place_ref[0, row]
+    for p in range(last):
+        for copy in far(p):
+            copy.wait_recv()
+    for way in range(2):
+        pick(theirs, handed, way, 0)
+        hand(way, 0).start()
     receive(last)
-    sends = []
-    for d in range(1, rows_count):
-        to = in_row(d)
-        chosen = place_ref[0, to]
-        for h in range(heads):
-            leaving[d, h] = finals[h, chosen]
-        send = pltpu.make_async_remote_copy(
-            leaving.at[d],
-            roll_hbm.at[row],
-            head_send.at[d],
-            head_recv.at[d],
-            device_id=(s, to),
-            device_id_type=mesh_id,
-        )
-        send.start()
-        sends.append(send)
-    chosen = place_ref[0, row]
-    for h in range(heads):
-        leaving[0, h] = finals[h, chosen]
-    keep = pltpu.make_async_copy(leaving.at[0], roll_hbm.at[row], own_sem)
-    keep.start()
-    finish(last - 1)
     finish(last)
     store = pltpu.make_async_copy(att, att_hbm, store_sem)
     store.start()
+    arriving = far(last)
+    for d in range(1, side):
+        for way in range(2):
+            arriving[2 * (d - 1) + way].wait_recv()
+            pick(theirs, handed, way, side - d)
+            hand(way, side - d).start()
+    for d in range(side):
+        for way in range(2):
+            pick(mine, picked, way, d)
+            keep(way, d).start()
     for p in range(prompts):
         swap(p).wait_send()
         for d in range(1, chips):
             spread(p, d).wait_send()
         give_back(p).wait_send()
-    for send in sends:
-        send.wait()
-    keep.wait()
+        for copy in near(p) + far(p):
+            copy.wait_send()
+    for d in range(side):
+        for way in range(2):
+            keep(way, d).wait()
+            hand(way, d).wait()
     store.wait()
 
 
@@ -623,6 +735,7 @@
     chains = prompts * heads
     units = UNROLL * heads
     nblk = tok // BLOCK
+    side = math.isqrt(rows_count)
     hbm = pl.BlockSpec(memory_space=pl.ANY)
     dma = pltpu.SemaphoreType.DMA
 
@@ -635,7 +748,7 @@
         out_specs=[hbm, hbm],
         out_shape=[
             jax.ShapeDtypeStruct((prompts, tok, width), BF16),
-            jax.ShapeDtypeStruct((rows_count, heads, DK, DV), BF16),
+            jax.ShapeDtypeStruct((side, side, heads, DK, DV), BF16),
         ],
         scratch_shapes=[
             pltpu.SMEM(lengths.shape, jnp.int32),
@@ -675,11 +788,15 @@
             pltpu.VMEM((heads, prompts, DK, DK + DV), BF16),
             pltpu.VMEM((prompts, DK, DK + DV), BF16),
             pltpu.VMEM((prompts, chips, DK, DK + DV), BF16),
-            pltpu.VMEM((prompts, 2, DK, DV), BF16),
-            pltpu.VMEM((prompts, 2, DK, DV), BF16),
+            pltpu.VMEM((prompts, DK, DV), BF16),
+            pltpu.VMEM((prompts, DK, DV), BF16),
             pltpu.VMEM((heads, prompts, DK, DV), BF16),
-            pltpu.VMEM((heads, prompts, DK, DV), BF16),
-            pltpu.VMEM((rows_count, heads, DK, DV), BF16),
+            pltpu.VMEM((prompts, side, side, DK // 2, DV), BF16),
+            pltpu.VMEM((prompts, side, side, DK // 2, DV), BF16),
+            pltpu.VMEM((2, side, side, DK // 2, DV), BF16),
+            pltpu.VMEM((2, side, side, DK // 2, DV), BF16),
+            pltpu.VMEM((8, 128), jnp.int32),
+            pltpu.VMEM((8, 128), jnp.int32),
             dma((prompts,)),
             dma((prompts,)),
             dma,
@@ -692,8 +809,14 @@
             dma((prompts, chips - 1)),
             dma((prompts,)),
             dma((prompts,)),
-            dma((rows_count,)),
-            dma((rows_count,)),
+            dma((prompts, 2, side - 1)),
+            dma((prompts, 2, side - 1)),
+            dma((prompts, 2, side - 1)),
+            dma((prompts, 2, side - 1)),
+            dma((2, side)),
+            dma((2, side)),
+            dma((2, side)),
+            dma,
             dma,
             dma((7,)),
         ],

time: 56.6 us -> 56.3 us (level)
  the two profiles are of different devices: /device:TPU:101 before, /device:TPU:1 now
where the time goes in v4:
time: 56.3 us; the launch traced here: 56.2 us
  Pallas kernels  52 us (92%)
  other arithmetic  3.55 us (6%)
  between operations  0.67 us (1%)
    pallas_call x1, Pallas kernels, delta(): pl.pallas_call(delta_kernel, in_specs=[hbm] * 10, out_specs=[hbm, hbm], o...  52 us
    select_n x1, other arithmetic, shards(): attended = jnp.where(position < limit, attended, 0).astype(BF16)  1.98 us
    reshape x1, other arithmetic, shards(): rollout = arrived.astype(F32).reshape(1, 1, head_count * heads, DK, DV)  1.56 us

profile of v4, /device:TPU:1, one launch (start us, length us, event | category | flops | bytes accessed | tf_op | source)
XLA Modules:
  0.0 56.2 jit_solution(1088101647855727145)
XLA Ops:
  0.6 0.0 copy-start
  0.7 52.0 %delta.1 = (bf16[4,1024,256]{2,1,0:T(8,128)(2,1)S(1)}, bf16[4,4,2,128,128]{4,3,2,1,0:T(8,128)(2,1)S(1)}) custom-call(s32[4]{0:T(128)} %len_hbm.1, s32[1,16]{1,0:T(1,128)} %place_hbm.1, bf16[4,2048,128]{2,1,0:T(8,128)(2,1)} %bitcast.5, bf16[4,1024,256]{2,1,0:T(8,128)(2,1)} %v_hbm.1, bf16[4,1024,256]{2,1,0:T(8,128)(2,1)} %z_hbm.1, bf16[4,2,128]{2,1,0:T(2,128)(2,1)} %cqk_hbm.1, ...), custom_call_target="tpu_custom_call" | custom-call | tf_op jit(solution)/shard_map/delta/pallas_call | solution.py:745
  52.7 0.0 copy-done
  52.7 2.0 %compare_select_fusion = bf16[4,1024,256]{2,1,0:T(8,128)(2,1)} fusion(bf16[4,1024,256]{2,1,0:T(8,128)(2,1)S(1)} %get-tuple-element.4, s32[4]{0:T(128)S(1)} %copy-done, s32[1024]{0:T(1024)S(1)} %iota_add_fusion), kind=kLoop, calls=%fused_computation | loop fusion | flops 2097152 | bytes 4198416 | tf_op jit(solution)/shard_map/jit(_where)/select_n | solution.py:862
  54.6 1.6 %convert.1 = f32[1,1,32,128,128]{4,3,2,1,0:T(8,128)} convert(bf16[1,1,32,128,128]{4,3,2,1,0:T(8,128)(2,1)S(1)} %bitcast.4) | non-fusion elementwise | flops 524288 | bytes 3145728 | tf_op jit(solution)/shard_map/reshape | solution.py:863
  (1 shorter events, 0.0 us)
Async XLA Ops:
  0.6 52.0 %copy-start = (s32[4]{0:T(128)S(1)}, s32[4]{0:T(128)}, u32[]{:S(2)}) copy-start(s32[4]{0:T(128)} %len_hbm.1) | copy-start | bytes 52
